TPU v7x, 128 devices: a whole 4x4x4 slice. The times are simulated.
128 devices in a mesh: expert: 16 (over y, z), etp: 4 (over x), dp: 2 (over core).
Axes of the slice: x: 4, y: 4, z: 4, core: 2. Of those that a mesh axis runs over, the one named last changes fastest.
Arguments:
- out_grad: bfloat16 [8192, 3072], P(('expert', 'dp')), may hold values from -6 to 6
- route: int32 [8192, 4], P(('expert', 'dp')), may hold values from 0 to 15, all different within a row; in each aligned block of 256 rows (0 to 255, 256 to 511, ...) at most 96 rows name the same one
- gate_prob: bfloat16 [8192, 4], P(('expert', 'dp')), may hold values from 0.049804688 to 0.59765625
- w_down: bfloat16 [16, 5376, 3072], P('expert', 'etp'), may hold values from -0.078125 to 0.078125
- gate_pre: bfloat16 [16, 3072, 5376], P('expert', 'dp', 'etp'), may hold values from -6 to 6
- up_pre: bfloat16 [16, 3072, 5376], P('expert', 'dp', 'etp'), may hold values from -6 to 6
Outputs:
- grad_gate: bfloat16 [16, 3072, 5376], P('expert', 'dp', 'etp')
- grad_up: bfloat16 [16, 3072, 5376], P('expert', 'dp', 'etp')
- grad_down: bfloat16 [16, 5376, 3072], P('expert', ('etp', 'dp'))
- grad_prob: float32 [8192, 4], P(('expert', 'dp'))
Inputs may be any that keep to these rules, and one draw needn't show every extreme that they name: `route`: each token names 4 different experts; among the 256 tokens of one device no expert is named more than 96 times, and in every draw some device names some expert exactly 96 times.
All inputs are finite; a program needn't handle non-finite values.
Results may differ from a plain program's by a relative error of at most 0.005.
Values may be sent and summed in bfloat16 or wider, within the bound.
No kernel may reach another device: no remote copies, remote signals or barrier semaphores. Data moves between devices by JAX's collectives and lax.ppermute only.
A program may use at most 192 MiB of HBM per device.

v0:
```python
import jax
import jax.numpy as jnp
from jax import lax
from jax.sharding import PartitionSpec as P


def local(out_grad, route, gate_prob, w_down, gate_pre, up_pre):
    tok_rows, width = out_grad.shape
    top_count = route.shape[1]
    groups = lax.axis_size("expert")
    slots = gate_pre.shape[1]
    capacity = slots // groups
    flat = route.reshape(-1)
    onehot = (flat[:, None] == jnp.arange(groups, dtype=jnp.int32)[None, :]).astype(jnp.int32)
    before = jnp.cumsum(onehot, axis=0) - onehot
    position = jnp.sum(before * onehot, axis=1)
    target = (flat * capacity + position).reshape(tok_rows, top_count)
    match = target[None, :, :] == jnp.arange(slots, dtype=jnp.int32)[:, None, None]
    dispatch = jnp.any(match, axis=2).astype(jnp.bfloat16)
    send_rows = jnp.dot(dispatch, out_grad, preferred_element_type=jnp.float32).astype(jnp.bfloat16)
    send_rows = send_rows.reshape(groups, capacity, width)
    send_prob = jnp.sum(
        jnp.where(match, gate_prob.astype(jnp.float32)[None, :, :], 0.0), axis=(1, 2)
    )
    send_prob = send_prob.astype(jnp.bfloat16).reshape(groups, capacity)
    recv_rows, recv_prob = (
        lax.all_to_all(send_rows, "expert", split_axis=0, concat_axis=0, tiled=True),
        lax.all_to_all(send_prob, "expert", split_axis=0, concat_axis=0, tiled=True),
    )
    rows = recv_rows.reshape(slots, width)
    prob = recv_prob.reshape(slots).astype(jnp.float32)[:, None]
    gate = gate_pre[0].astype(jnp.float32)
    upper = up_pre[0].astype(jnp.float32)
    raw = lax.dot_general(
        rows, w_down[0], (((1,), (1,)), ((), ())), preferred_element_type=jnp.float32
    )
    sig = jax.nn.sigmoid(gate)
    act = gate * sig * upper
    scaled_grad = prob * raw
    grad_up = (scaled_grad * (gate * sig)).astype(jnp.bfloat16)
    grad_gate = (scaled_grad * upper * (sig * (1.0 + gate * (1.0 - sig)))).astype(jnp.bfloat16)
    scaled = (prob * act).astype(jnp.bfloat16)
    partial_sum = jnp.sum(raw * act, axis=1).reshape(groups, capacity)
    grad_down = lax.psum_scatter(
        lax.dot_general(scaled, rows, (((0,), (0,)), ((), ())), preferred_element_type=jnp.float32),
        "dp",
        scatter_dimension=0,
        tiled=True,
    ).astype(jnp.bfloat16)
    summed = lax.psum(partial_sum, "etp")
    returned = lax.all_to_all(summed, "expert", split_axis=0, concat_axis=0, tiled=True)
    returned_flat = returned.reshape(slots)
    grad_prob = jnp.sum(jnp.where(match, returned_flat[:, None, None], 0.0), axis=0)
    return (grad_gate[None], grad_up[None], grad_down[None], grad_prob)


def solution(mesh):
    in_specs = (
        P(("expert", "dp"), None),
        P(("expert", "dp"), None),
        P(("expert", "dp"), None),
        P("expert", "etp", None),
        P("expert", "dp", "etp"),
        P("expert", "dp", "etp"),
    )
    out_specs = (
        P("expert", "dp", "etp"),
        P("expert", "dp", "etp"),
        P("expert", ("etp", "dp"), None),
        P(("expert", "dp"), None),
    )
    return jax.shard_map(local, mesh=mesh, in_specs=in_specs, out_specs=out_specs, check_vma=False)
```

profile of v0, /device:TPU:1, one launch (start us, length us, event | category | flops | bytes accessed | tf_op | source)
XLA Modules:
  0.0 255.0 jit_solution(5946258623328460261)
XLA Ops:
  7.2 0.9 copy.37
  8.1 0.1 eq.42
  8.2 0.1 eq.38
  8.4 4.5 %reduce-window.6 = s32[16,8,128]{2,1,0:T(8,128)S(1)} reduce-window(s32[16,8,128]{2,1,0:T(8,128)S(1)} %fusion.31, s32[]{:T(128)} %constant.3.clone.1), window={size=1x1x128 pad=0_0x0_0x127_0}, to_apply=%region_0.0 | reduce-window | flops 2080768 | bytes 131076 | tf_op jit(solution)/shard_map/reduce-window
  12.9 0.1 slice.8
  13.0 0.1 copy.39
  13.1 0.1 copy.40
  13.2 0.1 broadcast_add_fusion
  13.3 0.1 reduce_sum.39
  13.5 0.1 copy.41
  13.6 0.7 multiply_add_fusion
  14.3 1.8 fusion.21
  16.1 2.8 %convolution_convert_fusion = bf16[1536,3072]{1,0:T(8,128)(2,1)S(1)} fusion(pred[1536,256]{1,0:T(8,128)(4,1)S(1)} %fusion.21, bf16[256,3072]{1,0:T(8,128)(2,1)S(1)} %copy-done), kind=kOutput, calls=%fused_computation.6 | convolution fusion | flops 2420637696 | bytes 11403264 | tf_op jit(solution)/shard_map/dot_general | solution.py:20
  18.9 114.8 %all_to_all.20 = bf16[16,96,3072]{2,1,0:T(8,128)(2,1)S(1)} all-to-all(bf16[16,96,3072]{2,1,0:T(8,128)(2,1)S(1)} %bitcast.84), channel_id=1, replica_groups=mesh['expert'=16,'etp'=4,'dp'=2] {'expert'}, dimensions={0} | all-to-all | bytes 18874368 | tf_op jit(solution)/shard_map/all_to_all | solution.py:27
  133.7 21.5 %fusion.8 = (f32[1536]{0:T(1024)S(1)}, f32[1536,1344]{0,1:T(8,128)}) fusion(bf16[1,1536,1344]{1,2,0:T(8,128)(2,1)S(1)} %copy-done.3, bf16[1,1536,1344]{1,2,0:T(8,128)(2,1)} %param.10, bf16[1536,3072]{1,0:T(8,128)(2,1)S(1)} %bitcast.85, bf16[1,1344,3072]{2,1,0:T(8,128)(2,1)} %param.9), kind=kOutput, calls=%fused_computation.14 | convolution fusion | flops 12702152704 | bytes 34215936 | tf_op jit(solution)/shard_map/dot_general | solution.py:34
  155.2 0.1 all_to_all.15
  155.3 9.3 %psum.7 = f32[16,1,96]{2,1,0:T(1,128)} all-reduce(f32[16,1,96]{2,1,0:T(1,128)S(1)} %all_to_all.15), channel_id=1, replica_groups=mesh['expert'=16,'etp'=4,'dp'=2] {'etp'}, use_global_device_ids=true, to_apply=%region_7.8 | all-reduce | flops 1536 | bytes 12288 | tf_op jit(solution)/shard_map/psum | solution.py:50
  164.6 4.5 %all-to-all-start.2 = ((f32[16,1,96]{2,1,0:T(1,128)}), f32[16,1,96]{2,1,0:T(1,128)S(1)}, u32[]{:S(2)}, u32[]{:S(2)}) async-start(f32[16,1,96]{2,1,0:T(1,128)} %psum.7), calls=%async_computation.3 | async-start | bytes 16384 | tf_op jit(solution)/shard_map/all_to_all | solution.py:51
  169.1 0.0 reduce-scatter.2.cloned.1.call-start
  169.1 6.3 %all-to-all-done.2 = f32[16,1,96]{2,1,0:T(1,128)S(1)} async-done(((f32[16,1,96]{2,1,0:T(1,128)}), f32[16,1,96]{2,1,0:T(1,128)S(1)}, u32[]{:S(2)}, u32[]{:S(2)}) %all-to-all-start.2) | async-done | bytes 6176 | tf_op jit(solution)/shard_map/all_to_all | solution.py:51
  175.4 0.5 broadcast.52
  175.9 0.7 reduce.7
  176.6 0.1 broadcast_in_dim.42
  176.7 2.3 select_reduce_fusion
  179.0 0.1 convert_element_type.93
  179.1 9.1 %all_to_all.21 = bf16[16,1,96]{2,1,0:T(2,128)(2,1)S(1)} all-to-all(bf16[16,1,96]{2,1,0:T(2,128)(2,1)S(1)} %convert_element_type.93), channel_id=1, replica_groups=mesh['expert'=16,'etp'=4,'dp'=2] {'expert'}, dimensions={0} | all-to-all | bytes 6144 | tf_op jit(solution)/shard_map/all_to_all | solution.py:28
  188.2 0.1 reshape.87
  188.3 23.0 %fusion.23 = f32[1344,3072]{1,0:T(8,128)} fusion(bf16[1536,3072]{1,0:T(8,128)(2,1)} %bitcast.86, bf16[1,1536,1344]{1,2,0:T(8,128)(2,1)} %param.11, bf16[1,1536,1344]{1,2,0:T(8,128)(2,1)} %param.10, f32[1536]{0:T(1024)S(1)} %reshape.87), kind=kOutput, calls=%fused_computation.33 | convolution fusion | flops 12702154752 | bytes 34215936 | tf_op jit(solution)/shard_map/dot_general | solution.py:45
  211.3 0.0 reduce-scatter.2.cloned.1.call-update
  211.3 10.0 %fusion.22 = (bf16[1,1536,1344]{1,2,0:T(8,128)(2,1)}, bf16[1,1536,1344]{1,2,0:T(8,128)(2,1)}) fusion(f32[1536,1344]{0,1:T(8,128)} %get-tuple-element.9, f32[1536]{0:T(1024)S(1)} %reshape.87, bf16[1,1536,1344]{1,2,0:T(8,128)(2,1)} %param.10, bf16[1,1536,1344]{1,2,0:T(8,128)(2,1)} %param.11), kind=kLoop, calls=%fused_computation.32 | loop fusion | flops 33030144 | bytes 24778752 | tf_op jit(solution)/shard_map/broadcast_in_dim | solution.py:54
  221.3 20.9 %reduce-scatter.2.cloned.1.call-done = f32[672,3072]{1,0:T(8,128)} async-done(((f32[1344,3072]{1,0:T(8,128)}), f32[672,3072]{1,0:T(8,128)}) %reduce-scatter.2.cloned.1.call-update) | async-done | bytes 8257552 | tf_op jit(solution)/shard_map/reduce_scatter | solution.py:44
  242.2 6.0 %convert_bitcast_fusion.2 = bf16[1,672,3072]{2,1,0:T(8,128)(2,1)} fusion(f32[672,3072]{1,0:T(8,128)} %reduce-scatter.2.cloned.1.call-done), kind=kLoop, calls=%fused_computation.35 | loop fusion | flops 2064384 | bytes 12386304 | tf_op jit(solution)/shard_map/broadcast_in_dim | solution.py:54
  (16 shorter events, 0.1 us)
Async XLA Ops:
  7.2 8.9 %copy-start = (bf16[256,3072]{1,0:T(8,128)(2,1)S(1)}, bf16[256,3072]{1,0:T(8,128)(2,1)}, u32[]{:S(2)}) copy-start(bf16[256,3072]{1,0:T(8,128)(2,1)} %param.6) | copy-start | bytes 4718596
  18.9 114.8 %copy-start.3 = (bf16[1,1536,1344]{1,2,0:T(8,128)(2,1)S(1)}, bf16[1,1536,1344]{1,2,0:T(8,128)(2,1)}, u32[]{:S(2)}) copy-start(bf16[1,1536,1344]{1,2,0:T(8,128)(2,1)} %param.11) | copy-start | bytes 12386308
  133.7 21.5 %copy-start.2 = (bf16[16,96,3072]{2,1,0:T(8,128)(2,1)}, bf16[16,96,3072]{2,1,0:T(8,128)(2,1)S(1)}, u32[]{:S(2)}) copy-start(bf16[16,96,3072]{2,1,0:T(8,128)(2,1)S(1)} %all_to_all.20) | copy-start | bytes 28311556
  133.7 35.4 %copy-start.4 = (bf16[256,4]{0,1:T(4,128)(2,1)S(1)}, bf16[256,4]{0,1:T(4,128)(2,1)}, u32[]{:S(2)}) copy-start(bf16[256,4]{0,1:T(4,128)(2,1)} %param.8) | copy-start | bytes 6148
  164.6 10.8 %all-to-all-start.2 = ((f32[16,1,96]{2,1,0:T(1,128)}), f32[16,1,96]{2,1,0:T(1,128)S(1)}, u32[]{:S(2)}, u32[]{:S(2)}) async-start(f32[16,1,96]{2,1,0:T(1,128)} %psum.7), calls=%async_computation.3 | async-start | bytes 16384 | tf_op jit(solution)/shard_map/all_to_all | solution.py:51
  169.1 73.1 %reduce-scatter.2.cloned.1.call-start = ((), (), s32[]{:S(2)}) async-start(), calls=%async_computation.4 | async-start | bytes 24772608 | tf_op jit(solution)/shard_map/reduce_scatter | solution.py:44
  211.3 36.8 %copy-start.1 = (bf16[256,3072]{1,0:T(8,128)(2,1)S(1)}, bf16[256,3072]{1,0:T(8,128)(2,1)}, u32[]{:S(2)}) copy-start(bf16[256,3072]{1,0:T(8,128)(2,1)} %param.6) | copy-start | bytes 4718596
Sparse Core Ops, SparseCore 0:
  211.4 30.7 reduce-scatter.1
where the time goes:
time: 255 us
  blocking collectives  133 us (52%)
  matrix products  47.3 us (19%)
  waiting for transfers between devices  27.2 us (11%)
  other arithmetic  26.1 us (10%)
  between operations  14.2 us (6%)
  starting transfers between devices  4.5 us (2%)
    all_to_all x1, blocking collectives, local(): lax.all_to_all(send_rows, 'expert', split_axis=0, concat_axis=0, tiled=True)  115 us
    dot_general x1, matrix products, local(): lax.dot_general(scaled, rows, (((0,), (0,)), ((), ())), preferred_element...  23 us
    dot_general x1, matrix products, local(): lax.dot_general(rows, w_down[0], (((1,), (1,)), ((), ())), preferred_elem...  21.5 us
    reduce_scatter x1, waiting for transfers between devices, local(): lax.psum_scatter(lax.dot_general(scaled, rows, (((0,), (0,)), ((), ())),...  20.9 us
    broadcast_in_dim x2, other arithmetic, local(): return (grad_gate[None], grad_up[None], grad_down[None], grad_prob)  15.9 us
    psum x1, blocking collectives, local(): summed = lax.psum(partial_sum, 'etp')  9.31 us
    all_to_all x1, blocking collectives, local(): lax.all_to_all(send_prob, 'expert', split_axis=0, concat_axis=0, tiled=True)  9.11 us
    all_to_all x1, waiting for transfers between devices, local(): lax.all_to_all(summed, 'expert', split_axis=0, concat_axis=0, tiled=True)  6.26 us
  transfers between devices with their start and end apart: 2, of which 2 were waited for; matrix products, arithmetic and copies ran while one was open for 4% of the time, Pallas kernels for 0%

commit v1 on v0

v1 whole, which is shorter than its diff:
```python
import functools

import jax
import jax.numpy as jnp
from jax import lax
from jax.experimental import pallas as pl
from jax.experimental.pallas import tpu as pltpu
from jax.sharding import PartitionSpec as P

BF16 = jnp.bfloat16
F32 = jnp.float32
LANES = 128
CHUNKS = ((0, 32), (32, 32), (64, 32))
TILE_FF = 256
TILE_D = 512


def params(megabytes):
    return pltpu.CompilerParams(
        dimension_semantics=("arbitrary",), vmem_limit_bytes=megabytes << 20
    )


def cost(flops, moved):
    return pl.CostEstimate(flops=flops, bytes_accessed=moved, transcendentals=0)


def dispatch_kernel(experts, chunks, where_ref, route_ref, prob_ref, grad_ref, *refs):
    outs, slot_ref, pick = refs[: len(chunks)], refs[len(chunks)], refs[len(chunks) + 1]
    tokens = route_ref.shape[0]
    half = grad_ref.shape[1]
    expert = lax.broadcasted_iota(jnp.int32, (tokens, LANES), 1)
    chosen = jnp.zeros((tokens, LANES), F32)
    prob = jnp.zeros((tokens, LANES), F32)
    for k in range(route_ref.shape[1]):
        hit = route_ref[:, k : k + 1] == expert
        chosen = jnp.where(hit, 1.0, chosen)
        prob = jnp.where(hit, prob_ref[:, k : k + 1].astype(F32), prob)
    chosen = chosen.astype(BF16)
    row = lax.broadcasted_iota(jnp.int32, (tokens, tokens), 0)
    col = lax.broadcasted_iota(jnp.int32, (tokens, tokens), 1)
    earlier = (row < col).astype(BF16)
    same = (row == col).astype(BF16)
    lower = (col < row).astype(BF16)
    over_rows = (((0,), (0,)), ((), ()))
    before_t = lax.dot_general(chosen, earlier, over_rows, preferred_element_type=F32)
    chosen_t = lax.dot_general(chosen, same, over_rows, preferred_element_type=F32)
    slot_t = jnp.where(chosen_t > 0.5, before_t, -1.0)
    slot_ref[...] = jnp.dot(lower, chosen, preferred_element_type=F32)
    prob = prob.astype(BF16)
    for (start, rows), out in zip(chunks, outs):
        place = lax.broadcasted_iota(jnp.int32, (rows, tokens), 0).astype(F32) + float(start)
        for e in range(experts):
            pick[pl.ds(e * rows, rows), :] = (slot_t[e : e + 1, :] == place).astype(BF16)
        chosen_rows = pick[pl.ds(0, experts * rows), :]
        out[:, :half] = jnp.dot(
            chosen_rows, grad_ref[...], preferred_element_type=F32
        ).astype(BF16)
        out[:, half:] = jnp.dot(chosen_rows, prob, preferred_element_type=F32).astype(BF16)


def dispatch(where, route, prob, grad, experts, chunks):
    tokens, width = grad.shape
    half = width // 2
    wide = half + LANES
    total = sum(rows for _, rows in chunks) * experts
    most = max(rows for _, rows in chunks) * experts
    return pl.pallas_call(
        functools.partial(dispatch_kernel, experts, chunks),
        out_shape=[jax.ShapeDtypeStruct((experts * r, wide), BF16) for _, r in chunks]
        + [jax.ShapeDtypeStruct((tokens, LANES), F32)],
        grid_spec=pltpu.PrefetchScalarGridSpec(
            num_scalar_prefetch=1,
            grid=(1,),
            in_specs=[
                pl.BlockSpec(route.shape, lambda i, w: (0, 0)),
                pl.BlockSpec(prob.shape, lambda i, w: (0, 0)),
                pl.BlockSpec((tokens, half), lambda i, w: (0, w[0])),
            ],
            out_specs=[pl.BlockSpec((experts * r, wide), lambda i, w: (0, 0)) for _, r in chunks]
            + [pl.BlockSpec((tokens, LANES), lambda i, w: (0, 0))],
            scratch_shapes=[pltpu.VMEM((most, tokens), BF16)],
        ),
        compiler_params=params(24),
        cost_estimate=cost(2 * total * tokens * wide, 2 * (tokens * half + total * wide)),
        name="dispatch",
    )(where, route, prob, grad)


def hidden_kernel(ff, first, where_ref, own_ref, oth_ref, wown_ref, woth_ref, gate_ref, up_ref, *refs):
    gg_ref, gu_ref, sct_ref, part_ref, acc = refs if first else refs[2:]
    n = pl.program_id(0)
    groups, rows, _ = gate_ref.shape
    tile = gate_ref.shape[2]
    half = oth_ref.shape[2] - LANES
    lane = lax.broadcasted_iota(jnp.int32, (1, LANES), 1)
    valid = lax.broadcasted_iota(jnp.int32, (1, tile), 1) + n * tile < ff
    by_col = (((1,), (1,)), ((), ()))

    @pl.when(n == 0)
    def _():
        acc[...] = jnp.zeros_like(acc)

    step = max(1, 128 // rows)
    for g in range(0, groups, step):
        size = step * rows
        own = own_ref[g : g + step].reshape(size, half + LANES)
        oth = oth_ref[g : g + step].reshape(size, half + LANES)
        raw = lax.dot_general(own[:, :half], wown_ref[...], by_col, preferred_element_type=F32)
        raw += lax.dot_general(oth[:, :half], woth_ref[...], by_col, preferred_element_type=F32)
        weight = jnp.sum(
            jnp.where(lane == where_ref[1], own[:, half:].astype(F32), 0.0), axis=1, keepdims=True
        )
        gate = gate_ref[g : g + step].reshape(size, tile).astype(F32)
        upper = up_ref[g : g + step].reshape(size, tile).astype(F32)
        sig = 0.5 * jnp.tanh(0.5 * gate) + 0.5
        gs = gate * sig
        act = gs * upper
        scaled_grad = weight * raw
        gu_ref[g : g + step] = (scaled_grad * gs).astype(BF16).reshape(step, rows, tile)
        gg_ref[g : g + step] = (
            (scaled_grad * upper * (sig + gs * (1.0 - sig))).astype(BF16).reshape(step, rows, tile)
        )
        sct_ref[:, g * rows : g * rows + size] = (weight * act).astype(BF16).T
        term = jnp.where(valid, raw * act, 0.0)
        total = term[:, :LANES]
        for at in range(LANES, tile, LANES):
            total += term[:, at : at + LANES]
        acc[g * rows : g * rows + size, :] += total

    @pl.when(n == pl.num_programs(0) - 1)
    def _():
        part_ref[...] = jnp.sum(acc[...].reshape(groups, rows, LANES), axis=2)


def hidden(where, own, oth, w, gate, up, before, chunk):
    start, rows = chunk
    groups, capacity, ff = gate.shape
    width = w.shape[1]
    half = width // 2
    size = groups * rows
    at = start // rows
    block = (groups, rows, TILE_FF)
    spec = pl.BlockSpec(block, lambda n, s: (0, at, n))
    whole = pl.BlockSpec(own.shape, lambda n, s: (0, 0, 0))
    first = before is None
    return pl.pallas_call(
        functools.partial(hidden_kernel, ff, first),
        out_shape=[
            jax.ShapeDtypeStruct(gate.shape, BF16),
            jax.ShapeDtypeStruct(gate.shape, BF16),
            jax.ShapeDtypeStruct((ff, size), BF16),
            jax.ShapeDtypeStruct((groups, rows), F32),
        ],
        grid_spec=pltpu.PrefetchScalarGridSpec(
            num_scalar_prefetch=1,
            grid=(pl.cdiv(ff, TILE_FF),),
            in_specs=[
                whole,
                whole,
                pl.BlockSpec((TILE_FF, half), lambda n, s: (n, s[0])),
                pl.BlockSpec((TILE_FF, half), lambda n, s: (n, 1 - s[0])),
                spec,
                spec,
            ]
            + ([] if first else [pl.BlockSpec(memory_space=pl.ANY)] * 2),
            out_specs=[
                spec,
                spec,
                pl.BlockSpec((TILE_FF, size), lambda n, s: (n, 0)),
                pl.BlockSpec((groups, rows), lambda n, s: (0, 0)),
            ],
            scratch_shapes=[pltpu.VMEM((size, LANES), F32)],
        ),
        input_output_aliases={} if first else {7: 0, 8: 1},
        compiler_params=params(32),
        cost_estimate=cost(2 * size * ff * width, 2 * (ff * width + size * width + 5 * size * ff)),
        name="hidden",
    )(where, own, oth, w, w, gate, up, *(() if first else before))


def down_kernel(count, fused, where_ref, *refs):
    total = jnp.dot(refs[0][...], refs[count][...], preferred_element_type=F32)
    for c in range(1, count):
        total += jnp.dot(refs[c][...], refs[count + c][...], preferred_element_type=F32)
    if fused:
        total += refs[2 * count][...].astype(F32)
    refs[-1][...] = total.astype(BF16)


def down(where, scaled, rows, mine, own_cols, got=None, into=None):
    count = len(scaled)
    ff = scaled[0].shape[0]
    half_ff = ff // 2
    wide = rows[0].shape[1]
    half = wide - LANES
    tiles = half // TILE_D
    fused = got is not None
    pick = (lambda i, s: (s[2], 0)) if mine else (lambda i, s: (1 - s[2], 0))
    in_specs = [pl.BlockSpec((half_ff, s.shape[1]), pick) for s in scaled]
    in_specs += [pl.BlockSpec((r.shape[0], TILE_D), lambda i, s: (0, i)) for r in rows]
    args = [where, *scaled, *rows]
    aliases = {}
    if fused:
        in_specs.append(pl.BlockSpec((half_ff, TILE_D), lambda i, s: (0, i)))
        args.append(got)
        if own_cols:
            out_spec = pl.BlockSpec((half_ff, TILE_D), lambda i, s: (0, s[0] * tiles + i))
        else:
            out_spec = pl.BlockSpec((half_ff, TILE_D), lambda i, s: (0, (1 - s[0]) * tiles + i))
        if into is not None:
            in_specs.append(pl.BlockSpec(memory_space=pl.ANY))
            aliases = {len(args): 0}
            args.append(into)
        out_cols = 2 * half
    else:
        out_spec = pl.BlockSpec((half_ff, TILE_D), lambda i, s: (0, i))
        out_cols = half
    depth = sum(s.shape[1] for s in scaled)
    return pl.pallas_call(
        functools.partial(down_kernel, count, fused),
        out_shape=jax.ShapeDtypeStruct((half_ff, out_cols), BF16),
        grid_spec=pltpu.PrefetchScalarGridSpec(
            num_scalar_prefetch=1, grid=(tiles,), in_specs=in_specs, out_specs=out_spec
        ),
        input_output_aliases=aliases,
        compiler_params=params(32),
        cost_estimate=cost(
            2 * half_ff * half * depth, 2 * (half_ff * half * 2 + depth * (half + half_ff))
        ),
        name="down",
    )(*args)


def combine_kernel(experts, route_ref, slot_ref, *refs):
    out_ref = refs[-1]
    values = refs[0][...]
    for ref in refs[1:-1]:
        values += ref[...]
    tokens = route_ref.shape[0]
    capacity = values.shape[1]
    place = lax.broadcasted_iota(jnp.int32, (tokens, capacity), 1).astype(F32)
    route = route_ref[...]
    total = jnp.zeros(route.shape, F32)
    for e in range(experts):
        hit = slot_ref[:, e : e + 1] == place
        mine = jnp.sum(jnp.where(hit, values[e : e + 1, :], 0.0), axis=1, keepdims=True)
        total = jnp.where(route == e, mine, total)
    out_ref[...] = total


def combine(route, slot, values):
    experts = values[0].shape[0]
    return pl.pallas_call(
        functools.partial(combine_kernel, experts),
        out_shape=jax.ShapeDtypeStruct(route.shape, F32),
        name="combine",
    )(route, slot, *values)


def local(out_grad, route, gate_prob, w_down, gate_pre, up_pre):
    experts = lax.axis_size("expert")
    etp = lax.axis_size("etp")
    slots, ff = gate_pre.shape[1:]
    capacity = slots // experts
    width = out_grad.shape[1]
    half = width // 2
    wide = half + LANES
    where = jnp.stack(
        [lax.axis_index("etp") % 2, lax.axis_index("expert"), lax.axis_index("dp")]
    ).astype(jnp.int32)
    *sends, slot = dispatch(where, route, gate_prob, out_grad, experts, CHUNKS)
    swap = [(2 * i, 2 * ((i - 1) % etp)) for i in range(etp)]
    swap += [(2 * i + 1, 2 * ((i + 1) % etp) + 1) for i in range(etp)]
    gate = gate_pre.reshape(experts, capacity, ff)
    up = up_pre.reshape(experts, capacity, ff)
    before = None
    own_rows, oth_rows, scaled, parts = [], [], [], []
    for chunk, send in zip(CHUNKS, sends):
        rows = chunk[1]
        own = lax.all_to_all(
            send.reshape(experts, rows, wide), "expert", split_axis=0, concat_axis=0, tiled=True
        )
        oth = lax.ppermute(own, ("etp", "dp"), swap)
        *before, sct, part = hidden(where, own, oth, w_down[0], gate, up, before, chunk)
        own_rows.append(own.reshape(experts * rows, wide))
        oth_rows.append(oth.reshape(experts * rows, wide))
        scaled.append(sct)
        parts.append(part)
    partial_sum = jnp.concatenate(parts, axis=1)
    back = lax.all_to_all(partial_sum, "expert", split_axis=0, concat_axis=0, tiled=True)
    others = [
        lax.ppermute(back, "etp", [(i, (i + k) % etp) for i in range(etp)]) for k in range(1, etp)
    ]
    other = [(0, 1), (1, 0)]
    got_own = lax.ppermute(down(where, scaled, own_rows, False, True), "dp", other)
    got_oth = lax.ppermute(down(where, scaled, oth_rows, False, False), "dp", other)
    grad_down = down(where, scaled, own_rows, True, True, got_own)
    grad_down = down(where, scaled, oth_rows, True, False, got_oth, grad_down)
    grad_prob = combine(route, slot, [back, *others])
    grad_gate, grad_up = before
    return (
        grad_gate.reshape(gate_pre.shape),
        grad_up.reshape(up_pre.shape),
        grad_down[None],
        grad_prob,
    )


def solution(mesh):
    in_specs = (
        P(("expert", "dp"), None),
        P(("expert", "dp"), None),
        P(("expert", "dp"), None),
        P("expert", "etp", None),
        P("expert", "dp", "etp"),
        P("expert", "dp", "etp"),
    )
    out_specs = (
        P("expert", "dp", "etp"),
        P("expert", "dp", "etp"),
        P("expert", ("etp", "dp"), None),
        P(("expert", "dp"), None),
    )
    return jax.shard_map(local, mesh=mesh, in_specs=in_specs, out_specs=out_specs, check_vma=False)
```

time: 255 us -> 246 us (0.965); the launches traced: 255 us -> 243 us
  Pallas kernels: 0 us -> 86.5 us
  blocking collectives: 133 us -> 66.2 us
  local copies, waits for them, and re-layouts: 2.51 us -> 54.7 us
  matrix products: 47.3 us -> 0 us
  other arithmetic: 26.1 us -> 0.16 us
  between operations: 14.2 us -> 0.83 us
  starting transfers between devices: 4.5 us -> 16 us
  waiting for transfers between devices: 27.2 us -> 18.6 us
    pallas_call x0 -> x9, Pallas kernels: none -> 86.5 us  [the longest x3 52.8 us: hidden(): pl.pallas_call(functools.partial(hidden_kernel, ff, first), out_shape=[ja...]
    all_to_all x2 -> x3, blocking collectives: 124 us -> 66.2 us  [the longest x2 56.6 us: local(): lax.all_to_all(send.reshape(experts, rows, wide), 'expert', split_axis=0,...]
    unnamed x11 -> x57, local copies, waits for them, and re-layouts: 0.96 us -> 54.7 us
    dot_general x3 -> x0, matrix products: 47.3 us -> none  [the longest x1 23 us: local(): lax.dot_general(scaled, rows, (((0,), (0,)), ((), ())), preferred_element...]
    reduce_scatter x1 -> x0, waiting for transfers between devices: 20.9 us -> none  [local(): lax.psum_scatter(lax.dot_general(scaled, rows, (((0,), (0,)), ((), ())),...]
    broadcast_in_dim x2 -> x0, other arithmetic: 15.9 us -> none  [local(): return (grad_gate[None], grad_up[None], grad_down[None], grad_prob)]
    all_to_all x1, waiting for transfers between devices: 6.26 us -> 18.6 us  [local(): lax.all_to_all(send.reshape(experts, rows, wide), 'expert', split_axis=0,...]
    ppermute x0 -> x8, starting transfers between devices: none -> 11.5 us  [the longest x1 6.35 us: local(): lax.ppermute(down(where, scaled, own_rows, False, True), 'dp', other)]
  transfers between devices with their start and end apart: 2 -> 9, of which waited for: 2 -> 1; matrix products, arithmetic and copies ran while one was open for 4% -> 11% of each run, Pallas kernels for 0% -> 21%
where the time goes in v1:
time: 246 us; the launch traced here: 243 us
  Pallas kernels  86.5 us (35%)
  blocking collectives  66.2 us (27%)
  local copies, waits for them, and re-layouts  54.7 us (22%)
  waiting for transfers between devices  18.6 us (8%)
  starting transfers between devices  16 us (7%)
    all_to_all x2, blocking collectives, local(): lax.all_to_all(send.reshape(experts, rows, wide), 'expert', split_axis=0,...  56.6 us
    unnamed x57, local copies, waits for them, and re-layouts  54.7 us
    pallas_call x3, Pallas kernels, hidden(): pl.pallas_call(functools.partial(hidden_kernel, ff, first), out_shape=[ja...  52.8 us
    pallas_call x4, Pallas kernels, down(): pl.pallas_call(functools.partial(down_kernel, count, fused), out_shape=ja...  27.4 us
    all_to_all x1, waiting for transfers between devices, local(): lax.all_to_all(send.reshape(experts, rows, wide), 'expert', split_axis=0,...  18.6 us
    all_to_all x1, blocking collectives, local(): lax.all_to_all(partial_sum, 'expert', split_axis=0, concat_axis=0, tiled=...  9.62 us
    ppermute x1, starting transfers between devices, local(): lax.ppermute(down(where, scaled, own_rows, False, True), 'dp', other)  6.35 us
  transfers between devices with their start and end apart: 9, of which 1 were waited for; matrix products, arithmetic and copies ran while one was open for 11% of the time, Pallas kernels for 21%

profile of v1, /device:TPU:1, one launch (start us, length us, event | category | flops | bytes accessed | tf_op | source)
XLA Modules:
  0.0 243.0 jit_solution(9037602869219509154)
XLA Ops:
  2.4 1.4 copy-done.18
  3.8 2.7 %dispatch.1 = (bf16[512,1664]{1,0:T(8,128)(2,1)S(1)}, bf16[512,1664]{1,0:T(8,128)(2,1)S(1)}, bf16[512,1664]{1,0:T(8,128)(2,1)S(1)}, f32[256,128]{1,0:T(8,128)S(1)}) custom-call(s32[3]{0:T(128)S(1)} %pad_add_fusion.where_ref, s32[256,4]{1,0:T(8,128)S(1)} %copy.23.route_ref, bf16[256,4]{1,0:T(8,128)(2,1)S(1)} %copy.24.prob_ref, bf16[256,3072]{1,0:T(8,128)(2,1)S(1)} %copy-done.18), custom_call_target="tpu_custom_call" | custom-call | flops 1308622848 | bytes 5898240 | tf_op jit(solution)/shard_map/dispatch/pallas_call | solution.py:68
  6.6 31.4 %all_to_all.26.own_ref = bf16[16,32,1664]{2,1,0:T(8,128)(2,1)S(1)} all-to-all(bf16[16,32,1664]{2,1,0:T(8,128)(2,1)S(1)} %bitcast.38), channel_id=1, replica_groups=mesh['expert'=16,'etp'=4,'dp'=2] {'expert'}, dimensions={0} | all-to-all | bytes 3407872 | tf_op jit(solution)/shard_map/all_to_all | solution.py:281
  38.0 25.2 %all_to_all.27.own_ref = bf16[16,32,1664]{2,1,0:T(8,128)(2,1)S(1)} all-to-all(bf16[16,32,1664]{2,1,0:T(8,128)(2,1)S(1)} %bitcast.37), channel_id=1, replica_groups=mesh['expert'=16,'etp'=4,'dp'=2] {'expert'}, dimensions={0} | all-to-all | bytes 3407872 | tf_op jit(solution)/shard_map/all_to_all | solution.py:281
  63.2 4.4 %all-to-all-start = ((bf16[16,32,1664]{2,1,0:T(8,128)(2,1)}), bf16[16,32,1664]{2,1,0:T(8,128)(2,1)}, u32[]{:S(2)}, u32[]{:S(2)}) async-start(bf16[16,32,1664]{2,1,0:T(8,128)(2,1)} %bitcast.36), calls=%async_computation | async-start | bytes 3407872 | tf_op jit(solution)/shard_map/all_to_all | solution.py:281
  70.1 18.6 %all-to-all-done.own_ref = bf16[16,32,1664]{2,1,0:T(8,128)(2,1)} async-done(((bf16[16,32,1664]{2,1,0:T(8,128)(2,1)}), bf16[16,32,1664]{2,1,0:T(8,128)(2,1)}, u32[]{:S(2)}, u32[]{:S(2)}) %all-to-all-start) | async-done | bytes 1703968 | tf_op jit(solution)/shard_map/all_to_all | solution.py:281
  89.9 6.5 %copy.25 = bf16[1,1536,1344]{2,1,0:T(8,128)(2,1)} copy(bf16[1,1536,1344]{1,2,0:T(8,128)(2,1)} %param.10) | data formatting | bytes 8257536 | tf_op args[4]
  96.4 6.4 %copy.26 = bf16[1,1536,1344]{2,1,0:T(8,128)(2,1)} copy(bf16[1,1536,1344]{1,2,0:T(8,128)(2,1)} %param.11) | data formatting | bytes 8257536 | tf_op args[5]
  102.8 2.2 copy-done
  105.1 2.2 copy-done.1
  107.3 17.6 %hidden.3 = (bf16[16,96,1344]{2,1,0:T(8,128)(2,1)S(1)}, bf16[16,96,1344]{2,1,0:T(8,128)(2,1)S(1)}, bf16[1344,512]{1,0:T(8,128)(2,1)S(1)}, f32[16,32]{1,0:T(8,128)S(1)}) custom-call(s32[3]{0:T(128)S(1)} %pad_add_fusion.where_ref, bf16[16,32,1664]{2,1,0:T(8,128)(2,1)S(1)} %all_to_all.27.own_ref, bf16[16,32,1664]{2,1,0:T(8,128)(2,1)} %collective-permute-done.2.oth_ref, ...), custom_call_target="tpu_custom_call" | custom-call | flops 4227858432 | bytes 18284544 | tf_op jit(solution)/shard_map/hidden/pallas_call | solution.py:147
  124.9 2.0 copy-done.3
  126.9 2.1 copy-done.6
  129.0 2.7 %copy-done.2 = bf16[1,1536,1344]{2,1,0:T(8,128)(2,1)S(1)} copy-done((bf16[1,1536,1344]{2,1,0:T(8,128)(2,1)S(1)}, bf16[1,1536,1344]{2,1,0:T(8,128)(2,1)}, u32[]{:S(2)}) %copy-start.2) | copy-done | bytes 4128792
  131.7 2.2 copy-done.4
  133.9 2.2 copy-done.7
  136.2 17.4 %hidden.4 = (bf16[16,96,1344]{2,1,0:T(8,128)(2,1)S(1)}, bf16[16,96,1344]{2,1,0:T(8,128)(2,1)S(1)}, bf16[1344,512]{1,0:T(8,128)(2,1)S(1)}, f32[16,32]{1,0:T(8,128)S(1)}) custom-call(s32[3]{0:T(128)S(1)} %pad_add_fusion.where_ref, bf16[16,32,1664]{2,1,0:T(8,128)(2,1)S(1)} %all_to_all.26.own_ref, ...), custom_call_target="tpu_custom_call", output_to_operand_aliasing={{0}: (7, {}), {1}: (8, {})} | custom-call | flops 4227858432 | bytes 18284544 | tf_op jit(solution)/shard_map/hidden/pallas_call | solution.py:147
  153.5 17.9 %hidden.5 = (bf16[16,96,1344]{2,1,0:T(8,128)(2,1)S(1)}, bf16[16,96,1344]{2,1,0:T(8,128)(2,1)S(1)}, bf16[1344,512]{1,0:T(8,128)(2,1)S(1)}, f32[16,32]{1,0:T(8,128)S(1)}) custom-call(s32[3]{0:T(128)S(1)} %pad_add_fusion.where_ref, bf16[16,32,1664]{2,1,0:T(8,128)(2,1)} %all-to-all-done.own_ref, ...), custom_call_target="tpu_custom_call", output_to_operand_aliasing={{0}: (7, {}), {1}: (8, {})} | custom-call | flops 4227858432 | bytes 18284544 | tf_op jit(solution)/shard_map/hidden/pallas_call | solution.py:147
  171.4 2.0 copy-done.5
  173.5 2.1 copy-done.8
  175.5 6.4 %down.5 = bf16[672,1536]{1,0:T(8,128)(2,1)} custom-call(s32[3]{0:T(128)S(1)} %pad_add_fusion.where_ref, bf16[1344,512]{1,0:T(8,128)(2,1)S(1)} %get-tuple-element.29.refs_0_, bf16[1344,512]{1,0:T(8,128)(2,1)S(1)} %get-tuple-element.30.refs_1_, bf16[1344,512]{1,0:T(8,128)(2,1)S(1)} %get-tuple-element.31.refs_2_, bf16[512,1664]{1,0:T(8,128)(2,1)S(1)} %bitcast.34, ...), custom_call_target="tpu_custom_call" | custom-call | flops 3170893824 | bytes 10911744 | tf_op jit(solution)/shard_map/down/pallas_call | solution.py:220
  181.9 6.3 %collective-permute-start.4 = (bf16[672,1536]{1,0:T(8,128)(2,1)}, bf16[672,1536]{1,0:T(8,128)(2,1)}, u32[]{:S(2)}, u32[]{:S(2)}) collective-permute-start(bf16[672,1536]{1,0:T(8,128)(2,1)} %down.5), channel_id=1, source_target_pairs={{0,1},{1,0},{2,3},{3,2},{4,5},{5,4},{6,7},{7,6},{8,9},{9,8},{10,11... | collective-permute-start | bytes 6193160 | tf_op jit(solution)/shard_map/ppermute | solution.py:296
  188.3 6.9 %down.4 = bf16[672,1536]{1,0:T(8,128)(2,1)} custom-call(s32[3]{0:T(128)S(1)} %pad_add_fusion.where_ref, bf16[1344,512]{1,0:T(8,128)(2,1)S(1)} %get-tuple-element.29.refs_0_, bf16[1344,512]{1,0:T(8,128)(2,1)S(1)} %get-tuple-element.30.refs_1_, bf16[1344,512]{1,0:T(8,128)(2,1)S(1)} %get-tuple-element.31.refs_2_, bf16[512,1664]{1,0:T(8,128)(2,1)} %bitcast.11.refs_3_, ...), custom_call_target="tpu_custom_call" | custom-call | flops 3170893824 | bytes 10911744 | tf_op jit(solution)/shard_map/down/pallas_call | solution.py:220
  195.3 9.6 %all_to_all.28 = f32[16,1,96]{2,1,0:T(1,128)S(1)} all-to-all(f32[16,1,96]{2,1,0:T(1,128)S(1)} %bitcast.46), channel_id=1, replica_groups=mesh['expert'=16,'etp'=4,'dp'=2] {'expert'}, dimensions={0} | all-to-all | bytes 12288 | tf_op jit(solution)/shard_map/all_to_all | solution.py:291
  206.4 6.3 %copy.29 = bf16[1,1536,1344]{1,2,0:T(8,128)(2,1)} copy(bf16[1,1536,1344]{2,1,0:T(8,128)(2,1)} %bitcast.30) | data formatting | bytes 8257536
  212.8 6.3 %copy.30 = bf16[1,1536,1344]{1,2,0:T(8,128)(2,1)} copy(bf16[1,1536,1344]{2,1,0:T(8,128)(2,1)} %bitcast.31) | data formatting | bytes 8257536
  219.7 3.6 %combine.1 = f32[256,4]{1,0:T(8,128)} custom-call(s32[256,4]{1,0:T(8,128)} %copy-done.16, f32[256,128]{1,0:T(8,128)} %copy-done.17, f32[16,96]{1,0:T(8,128)} %bitcast.50, f32[16,96]{1,0:T(8,128)} %copy-done.22, f32[16,96]{1,0:T(8,128)} %copy-done.21, f32[16,96]{1,0:T(8,128)} %copy-done.20), custom_call_target="tpu_custom_call" | custom-call | tf_op jit(solution)/shard_map/combine/pallas_call | solution.py:254
  223.3 1.6 copy.31
  224.9 1.3 copy-done.10
  227.6 1.3 copy-done.14
  228.9 6.8 %down.6.refs_7_ = bf16[672,3072]{1,0:T(8,128)(2,1)} custom-call(s32[3]{0:T(128)S(1)} %pad_add_fusion.where_ref, bf16[1344,512]{1,0:T(8,128)(2,1)S(1)} %copy-done.10, bf16[1344,512]{1,0:T(8,128)(2,1)S(1)} %copy-done.12, bf16[1344,512]{1,0:T(8,128)(2,1)S(1)} %copy-done.14, bf16[512,1664]{1,0:T(8,128)(2,1)S(1)} %bitcast.35, bf16[512,1664]{1,0:T(8,128)(2,1)S(1)} %bitcast.33, ...), custom_call_target="tpu_custom_call" | custom-call | flops 3170893824 | bytes 10911744 | tf_op jit(solution)/shard_map/down/pallas_call | solution.py:220
  235.7 7.3 %down.7 = bf16[672,3072]{1,0:T(8,128)(2,1)} custom-call(s32[3]{0:T(128)S(1)} %pad_add_fusion.where_ref, bf16[1344,512]{1,0:T(8,128)(2,1)S(1)} %copy-done.10, bf16[1344,512]{1,0:T(8,128)(2,1)S(1)} %copy-done.12, bf16[1344,512]{1,0:T(8,128)(2,1)S(1)} %copy-done.14, bf16[512,1664]{1,0:T(8,128)(2,1)} %bitcast.11.refs_3_, ...), custom_call_target="tpu_custom_call", output_to_operand_aliasing={{}: (8, {})} | custom-call | flops 3170893824 | bytes 10911744 | tf_op jit(solution)/shard_map/down/pallas_call | solution.py:220
  (58 shorter events, 9.0 us)
Async XLA Ops:
  2.3 4.2 %copy-start.16 = (s32[256,4]{1,0:T(8,128)}, s32[256,4]{1,0:T(8,128)S(1)}, u32[]{:S(2)}) copy-start(s32[256,4]{1,0:T(8,128)S(1)} %copy.23.route_ref) | copy-start | bytes 12292
  2.4 1.4 copy-start.18
  6.5 56.6 %copy-start.15 = (bf16[512,1664]{1,0:T(8,128)(2,1)}, bf16[512,1664]{1,0:T(8,128)(2,1)S(1)}, u32[]{:S(2)}) copy-start(bf16[512,1664]{1,0:T(8,128)(2,1)S(1)} %get-tuple-element.20) | copy-start | bytes 5111812
  6.5 56.6 %copy-start.17 = (f32[256,128]{1,0:T(8,128)}, f32[256,128]{1,0:T(8,128)S(1)}, u32[]{:S(2)}) copy-start(f32[256,128]{1,0:T(8,128)S(1)} %get-tuple-element.32.slot_ref) | copy-start | bytes 393220
  63.2 25.5 %all-to-all-start = ((bf16[16,32,1664]{2,1,0:T(8,128)(2,1)}), bf16[16,32,1664]{2,1,0:T(8,128)(2,1)}, u32[]{:S(2)}, u32[]{:S(2)}) async-start(bf16[16,32,1664]{2,1,0:T(8,128)(2,1)} %bitcast.36), calls=%async_computation | async-start | bytes 3407872 | tf_op jit(solution)/shard_map/all_to_all | solution.py:281
  67.6 35.2 %collective-permute-start.2 = (bf16[16,32,1664]{2,1,0:T(8,128)(2,1)S(1)}, bf16[16,32,1664]{2,1,0:T(8,128)(2,1)}, u32[]{:S(2)}, u32[]{:S(2)}) collective-permute-start(bf16[16,32,1664]{2,1,0:T(8,128)(2,1)S(1)} %all_to_all.27.own_ref), channel_id=1, source_target_pairs={{0,6},{2,0},{4,2},{6,4},{1,3},{3,5},{5,7},{7,1},{8,14},{10,8},{12,... | collective-permute-start | bytes 5111816 | tf_op jit(solution)/shard_map/ppermute | solution.py:284
  68.9 60.1 %collective-permute-start.1 = (bf16[16,32,1664]{2,1,0:T(8,128)(2,1)S(1)}, bf16[16,32,1664]{2,1,0:T(8,128)(2,1)}, u32[]{:S(2)}, u32[]{:S(2)}) collective-permute-start(bf16[16,32,1664]{2,1,0:T(8,128)(2,1)S(1)} %all_to_all.26.own_ref), channel_id=1, source_target_pairs={{0,6},{2,0},{4,2},{6,4},{1,3},{3,5},{5,7},{7,1},{8,14},{10,8},{12,... | collective-permute-start | bytes 5111816 | tf_op jit(solution)/shard_map/ppermute | solution.py:284
  88.7 64.8 %collective-permute-start = (bf16[16,32,1664]{2,1,0:T(8,128)(2,1)}, bf16[16,32,1664]{2,1,0:T(8,128)(2,1)}, u32[]{:S(2)}, u32[]{:S(2)}) collective-permute-start(bf16[16,32,1664]{2,1,0:T(8,128)(2,1)} %all-to-all-done.own_ref), channel_id=1, source_target_pairs={{0,6},{2,0},{4,2},{6,4},{1,3},{3,5},{5,7},{7,1},{8,14},{10,8},{12,... | collective-permute-start | bytes 5111816 | tf_op jit(solution)/shard_map/ppermute | solution.py:284
  96.4 32.6 %slice-start = ((s8[4325376]{0:T(1024)(128)(4,1)}), s8[131072]{0:T(1024)(128)(4,1)S(1)}, s32[]{:S(2)}) async-start(s8[4325376]{0:T(1024)(128)(4,1)} %bitcast.23), calls=%async_computation.4 | async-start | bytes 262144
  102.8 2.2 copy-start
  105.1 2.2 copy-start.1
  107.3 21.7 %slice-start.1 = ((s8[4325376]{0:T(1024)(128)(4,1)}), s8[4194304]{0:T(1024)(128)(4,1)S(1)}, s32[]{:S(2)}) async-start(s8[4325376]{0:T(1024)(128)(4,1)} %bitcast.23), calls=%async_computation.5 | async-start | bytes 8388608
  124.9 2.0 copy-start.3
  126.9 2.1 copy-start.6
  129.0 59.3 %copy-start.9 = (bf16[1344,512]{1,0:T(8,128)(2,1)}, bf16[1344,512]{1,0:T(8,128)(2,1)S(1)}, u32[]{:S(2)}) copy-start(bf16[1344,512]{1,0:T(8,128)(2,1)S(1)} %get-tuple-element.29.refs_0_) | copy-start | bytes 4128772
  129.0 2.7 %copy-start.2 = (bf16[1,1536,1344]{2,1,0:T(8,128)(2,1)S(1)}, bf16[1,1536,1344]{2,1,0:T(8,128)(2,1)}, u32[]{:S(2)}) copy-start(bf16[1,1536,1344]{2,1,0:T(8,128)(2,1)} %copy.26) | copy-start | bytes 12386308
  131.7 2.2 copy-start.4
  133.9 2.2 copy-start.7
  153.5 34.8 %copy-start.11 = (bf16[1344,512]{1,0:T(8,128)(2,1)}, bf16[1344,512]{1,0:T(8,128)(2,1)S(1)}, u32[]{:S(2)}) copy-start(bf16[1344,512]{1,0:T(8,128)(2,1)S(1)} %get-tuple-element.30.refs_1_) | copy-start | bytes 4128772
  171.4 2.1 copy-start.5
  173.5 2.1 copy-start.8
  175.5 12.8 %copy-start.13 = (bf16[1344,512]{1,0:T(8,128)(2,1)}, bf16[1344,512]{1,0:T(8,128)(2,1)S(1)}, u32[]{:S(2)}) copy-start(bf16[1344,512]{1,0:T(8,128)(2,1)S(1)} %get-tuple-element.31.refs_2_) | copy-start | bytes 4128772
  181.9 43.0 %collective-permute-start.4 = (bf16[672,1536]{1,0:T(8,128)(2,1)}, bf16[672,1536]{1,0:T(8,128)(2,1)}, u32[]{:S(2)}, u32[]{:S(2)}) collective-permute-start(bf16[672,1536]{1,0:T(8,128)(2,1)} %down.5), channel_id=1, source_target_pairs={{0,1},{1,0},{2,3},{3,2},{4,5},{5,4},{6,7},{7,6},{8,9},{9,8},{10,11... | collective-permute-start | bytes 6193160 | tf_op jit(solution)/shard_map/ppermute | solution.py:296
  195.2 40.4 %collective-permute-start.3 = (bf16[672,1536]{1,0:T(8,128)(2,1)}, bf16[672,1536]{1,0:T(8,128)(2,1)}, u32[]{:S(2)}, u32[]{:S(2)}) collective-permute-start(bf16[672,1536]{1,0:T(8,128)(2,1)} %down.4), channel_id=1, source_target_pairs={{0,1},{1,0},{2,3},{3,2},{4,5},{5,4},{6,7},{7,6},{8,9},{9,8},{10,11... | collective-permute-start | bytes 6193160 | tf_op jit(solution)/shard_map/ppermute | solution.py:297
  204.9 7.8 %copy-start.19 = (f32[16,1,96]{2,1,0:T(1,128)}, f32[16,1,96]{2,1,0:T(1,128)S(1)}, u32[]{:S(2)}) copy-start(f32[16,1,96]{2,1,0:T(1,128)S(1)} %all_to_all.28) | copy-start | bytes 18436
  204.9 14.2 %collective-permute-start.7 = (f32[16,96]{1,0:T(8,128)S(1)}, f32[16,96]{1,0:T(8,128)S(1)}, u32[]{:S(2)}, u32[]{:S(2)}) collective-permute-start(f32[16,96]{1,0:T(8,128)S(1)} %bitcast.47), channel_id=1, source_target_pairs={{0,6},{2,0},{4,2},{6,4},{1,7},{3,1},{5,3},{7,5},{8,14},{10,8},{12,... | collective-permute-start | bytes 18440 | tf_op jit(solution)/shard_map/ppermute | solution.py:293
  205.5 13.6 %collective-permute-start.6 = (f32[16,96]{1,0:T(8,128)S(1)}, f32[16,96]{1,0:T(8,128)S(1)}, u32[]{:S(2)}, u32[]{:S(2)}) collective-permute-start(f32[16,96]{1,0:T(8,128)S(1)} %bitcast.48), channel_id=1, source_target_pairs={{0,4},{2,6},{4,0},{6,2},{1,5},{3,7},{5,1},{7,3},{8,12},{10,14},{12... | collective-permute-start | bytes 18440 | tf_op jit(solution)/shard_map/ppermute | solution.py:293
  205.7 13.4 %collective-permute-start.5 = (f32[16,96]{1,0:T(8,128)S(1)}, f32[16,96]{1,0:T(8,128)S(1)}, u32[]{:S(2)}, u32[]{:S(2)}) collective-permute-start(f32[16,96]{1,0:T(8,128)S(1)} %bitcast.49), channel_id=1, source_target_pairs={{0,2},{2,4},{4,6},{6,0},{1,3},{3,5},{5,7},{7,1},{8,10},{10,12},{12... | collective-permute-start | bytes 18440 | tf_op jit(solution)/shard_map/ppermute | solution.py:293
  219.1 0.6 copy-start.21
  224.9 1.3 copy-start.10
  226.2 1.3 copy-start.12
  227.6 1.3 copy-start.14
  (2 other events, 1.2 us)

commit v2 on v0

v2 whole, which is shorter than its diff:
```python
import functools

import jax
import jax.numpy as jnp
from jax import lax
from jax.experimental import pallas as pl
from jax.experimental.pallas import tpu as pltpu
from jax.sharding import PartitionSpec as P

BF16 = jnp.bfloat16
F32 = jnp.float32
LANES = 128
SHARED = ((0, 768), (1536, 512))
DIRECT = (2560, 512)
TILE_FF = 336
TILE_D = 256
SUB = 16
COLS = 256
VMEM_MB = 56
NT = (((1,), (1,)), ((), ()))


def params():
    return pltpu.CompilerParams(
        dimension_semantics=("arbitrary",), vmem_limit_bytes=VMEM_MB << 20
    )


def cost(flops, moved):
    flops, moved = flops // 4, moved // 4
    return pl.CostEstimate(flops=flops, bytes_accessed=moved, transcendentals=0)


def call(kernel, name, grid, in_specs, out_specs, out_shape, scratch, flops, moved, aliases=None):
    return pl.pallas_call(
        kernel,
        out_shape=out_shape,
        grid_spec=pltpu.PrefetchScalarGridSpec(
            num_scalar_prefetch=1,
            grid=grid,
            in_specs=in_specs,
            out_specs=out_specs,
            scratch_shapes=scratch,
        ),
        input_output_aliases=aliases or {},
        compiler_params=params(),
        cost_estimate=cost(flops, moved),
        name=name,
    )


def fixed(i, s):
    return (0, 0)


OWN, OTHER, SAME = 0, 1, 2


def column(chunk, side):
    first, size = chunk
    if side == SAME:
        return lambda s: first // size
    return lambda s: first // size + (s[0] if side == OWN else 1 - s[0])


def dispatch_kernel(experts, capacity, where_ref, route_ref, prob_ref, grad_ref,
                    send_ref, slot_ref, pick_ref):
    top, tokens = route_ref.shape
    expert = lax.broadcasted_iota(jnp.int32, (experts, tokens), 0)
    chosen = jnp.zeros((experts, tokens), F32)
    prob = jnp.zeros((experts, tokens), F32)
    for k in range(top):
        hit = route_ref[k : k + 1, :] == expert
        chosen = jnp.where(hit, 1.0, chosen)
        prob = jnp.where(hit, prob_ref[k : k + 1, :].astype(F32), prob)
    row = lax.broadcasted_iota(jnp.int32, (tokens, tokens), 0)
    col = lax.broadcasted_iota(jnp.int32, (tokens, tokens), 1)
    earlier = (row < col).astype(BF16)
    before = jnp.dot(chosen.astype(BF16), earlier, preferred_element_type=F32)
    slot = jnp.where(chosen > 0.5, before, -1.0)
    slot_ref[...] = slot
    place = lax.broadcasted_iota(jnp.int32, (capacity, tokens), 0).astype(F32)
    for e in range(experts):
        pick_ref[pl.ds(e * capacity, capacity), :] = jnp.where(
            slot[e : e + 1, :] == place, prob[e : e + 1, :], 0.0
        ).astype(BF16)
    send_ref[...] = jnp.dot(
        pick_ref[...], grad_ref[...], preferred_element_type=F32
    ).astype(BF16)


def dispatch(where, route, prob, grad, experts, capacity):
    tokens, width = grad.shape
    at = column(SHARED[0], OWN)
    part = SHARED[0][1]
    total = experts * capacity
    return call(
        functools.partial(dispatch_kernel, experts, capacity),
        "dispatch",
        (1,),
        [
            pl.BlockSpec(route.shape, fixed),
            pl.BlockSpec(prob.shape, fixed),
            pl.BlockSpec((tokens, part), lambda i, s: (0, at(s))),
        ],
        [
            pl.BlockSpec((total, part), fixed),
            pl.BlockSpec((experts, tokens), fixed),
            pl.BlockSpec((total, tokens), fixed),
        ],
        [
            jax.ShapeDtypeStruct((total, part), BF16),
            jax.ShapeDtypeStruct((experts, tokens), F32),
            jax.ShapeDtypeStruct((total, tokens), BF16),
        ],
        [],
        2 * total * tokens * part,
        2 * total * part,
    )(where, route, prob, grad)


def more_kernel(where_ref, pick_ref, grad_ref, send_ref):
    send_ref[...] = jnp.dot(
        pick_ref[...], grad_ref[...], preferred_element_type=F32
    ).astype(BF16)


def dispatch_more(where, pick, grad, chunk, side):
    total, tokens = pick.shape
    part = chunk[1]
    at = column(chunk, side)
    return call(
        more_kernel,
        "dispatch_more",
        (2,),
        [
            pl.BlockSpec((total // 2, tokens), lambda i, s: (i, 0)),
            pl.BlockSpec((tokens, part), lambda i, s: (0, at(s))),
        ],
        pl.BlockSpec((total // 2, part), lambda i, s: (i, 0)),
        jax.ShapeDtypeStruct((total, part), BF16),
        [],
        2 * total * tokens * part,
        2 * total * part,
    )(where, pick, grad)


def over_blocks(shape, body):
    def step(i, _):
        at = pl.ds(pl.multiple_of(i * SUB, SUB), SUB)
        for c in range(0, shape[1], COLS):
            body(at, pl.ds(c, COLS))
        return 0

    lax.fori_loop(0, shape[0] // SUB, step, 0)


def act_kernel(where_ref, gate_ref, up_ref, other_ref, mine_ref):
    def fill(out_ref):
        def body(at, cols):
            gate = gate_ref[at, cols].astype(F32)
            sig = 0.5 * jnp.tanh(0.5 * gate) + 0.5
            out_ref[at, cols] = (gate * sig * up_ref[at, cols].astype(F32)).astype(BF16)

        over_blocks(gate_ref.shape, body)

    @pl.when(pl.program_id(0) == 0)
    def _():
        fill(other_ref)

    @pl.when(pl.program_id(0) == 1)
    def _():
        fill(mine_ref)


def activation(where, gate, up):
    ff, slots = gate.shape
    tiles = ff // 2 // TILE_FF
    side = lambda h, s: h * s[2] + (1 - h) * (1 - s[2])
    spec = pl.BlockSpec((TILE_FF, slots), lambda h, n, s: (side(h, s) * tiles + n, 0))
    out = jax.ShapeDtypeStruct((ff // 2, slots), BF16)
    return pl.pallas_call(
        act_kernel,
        out_shape=[out, out],
        grid_spec=pltpu.PrefetchScalarGridSpec(
            num_scalar_prefetch=1,
            grid=(2, tiles),
            in_specs=[spec, spec],
            out_specs=[
                pl.BlockSpec((TILE_FF, slots), lambda h, n, s: (jnp.where(h == 0, n, tiles - 1), 0)),
                pl.BlockSpec((TILE_FF, slots), lambda h, n, s: (jnp.where(h == 0, 0, n), 0)),
            ],
        ),
        compiler_params=pltpu.CompilerParams(
            dimension_semantics=("arbitrary", "arbitrary"), vmem_limit_bytes=VMEM_MB << 20
        ),
        cost_estimate=cost(20 * ff * slots, 6 * ff * slots),
        name="activation",
    )(where, gate, up)


def piece_specs(pieces, slots):
    specs = []
    for _, chunk, side in pieces:
        at = column(chunk, side)
        specs.append(pl.BlockSpec((slots, chunk[1]), fixed))
        specs.append(pl.BlockSpec((TILE_FF, chunk[1]), lambda n, s, at=at: (n, at(s))))
    return specs


def piece_dots(refs, count):
    total = None
    for p in range(count):
        term = lax.dot_general(
            refs[2 * p + 1][...], refs[2 * p][...], NT, preferred_element_type=F32
        )
        total = term if total is None else total + term
    return total


def raw_kernel(count, more, where_ref, *refs):
    total = piece_dots(refs, count)
    if more:
        total += refs[2 * count][...]
    refs[-1][...] = total


def raw_part(where, w, pieces, before=None):
    slots = pieces[0][0].shape[0]
    ff, width = w.shape
    depth = sum(chunk[1] for _, chunk, _ in pieces)
    tile = pl.BlockSpec((TILE_FF, slots), lambda n, s: (n, 0))
    args = [x for rows, _, _ in pieces for x in (rows, w)]
    more = before is not None
    return call(
        functools.partial(raw_kernel, len(pieces), more),
        "raw",
        (ff // TILE_FF,),
        piece_specs(pieces, slots) + ([tile] if more else []),
        tile,
        jax.ShapeDtypeStruct((ff, slots), F32),
        [],
        2 * slots * ff * depth,
        2 * (ff + slots) * depth + 8 * ff * slots,
    )(where, *args, *([before] if more else []))


def finish_kernel(count, where_ref, gate_ref, up_ref, before_ref, *refs):
    gg_ref, gu_ref, part_ref, acc = refs[2 * count :]
    tile, slots = gate_ref.shape

    @pl.when(pl.program_id(0) == 0)
    def _():
        acc[...] = jnp.zeros_like(acc)

    for c in range(0, slots, COLS):
        cols = pl.ds(c, COLS)
        raw = before_ref[:, cols]
        for p in range(count):
            raw += lax.dot_general(
                refs[2 * p + 1][...], refs[2 * p][cols, :], NT, preferred_element_type=F32
            )
        total = jnp.zeros((8, COLS), F32)
        for r in range(0, tile, SUB):
            at = pl.ds(r, SUB)
            gate = gate_ref[at, cols].astype(F32)
            upper = up_ref[at, cols].astype(F32)
            value = raw[r : r + SUB]
            sig = 0.5 * jnp.tanh(0.5 * gate) + 0.5
            gs = gate * sig
            gu_ref[at, cols] = (value * gs).astype(BF16)
            gg_ref[at, cols] = (value * upper * (sig + gs * (1.0 - sig))).astype(BF16)
            term = value * (gs * upper)
            total += term[:8] + term[8:]
        acc[:, cols] += total

    @pl.when(pl.program_id(0) == pl.num_programs(0) - 1)
    def _():
        total = jnp.sum(acc[...], axis=0, keepdims=True)
        groups, capacity = part_ref.shape
        for g in range(groups):
            part_ref[g : g + 1, :] = total[:, g * capacity : (g + 1) * capacity]


def finish(where, gate, up, before, w, pieces, groups):
    ff, slots = gate.shape
    depth = sum(chunk[1] for _, chunk, _ in pieces)
    tile = pl.BlockSpec((TILE_FF, slots), lambda n, s: (n, 0))
    args = [x for rows, _, _ in pieces for x in (rows, w)]
    return call(
        functools.partial(finish_kernel, len(pieces)),
        "finish",
        (ff // TILE_FF,),
        [tile, tile, tile] + piece_specs(pieces, slots),
        [tile, tile, pl.BlockSpec((groups, slots // groups), fixed)],
        [
            jax.ShapeDtypeStruct((ff, slots), BF16),
            jax.ShapeDtypeStruct((ff, slots), BF16),
            jax.ShapeDtypeStruct((groups, slots // groups), F32),
        ],
        [pltpu.VMEM((8, slots), F32)],
        2 * slots * ff * depth,
        2 * (ff + slots) * depth + 12 * ff * slots,
    )(where, gate, up, before, *args)


def down_kernel(counts, where_ref, here_ref, there_ref, *refs):
    at = 0
    for p, count in enumerate(counts):

        @pl.when((pl.program_id(0) >= at) & (pl.program_id(0) < at + count))
        def _(p=p):
            total = jnp.dot(here_ref[...], refs[2 * p][...], preferred_element_type=F32)
            total += jnp.dot(there_ref[...], refs[2 * p + 1][...], preferred_element_type=F32)
            refs[-1][...] = total.astype(BF16)

        at += count


def down(where, acts, pieces, width, into=None):
    half_ff, slots = acts[0].shape
    counts = [chunk[1] // TILE_D for _, _, chunk, _ in pieces]
    tiles = sum(counts)
    in_specs = [pl.BlockSpec((half_ff, slots), fixed)] * 2
    args = [where, *acts]
    starts = []
    for p, (here, there, _, _) in enumerate(pieces):
        start = sum(counts[:p])
        starts.append(start)
        place = lambda i, s, a=start, n=counts[p]: (0, jnp.clip(i - a, 0, n - 1))
        in_specs += [pl.BlockSpec((slots, TILE_D), place)] * 2
        args += [here, there]

    def place_out(i, s):
        at = 0
        for (_, _, chunk, side), start, count in zip(pieces, starts, counts):
            first = column(chunk, side)(s) * count
            at = jnp.where((i >= start) & (i < start + count), first + i - start, at)
        return (0, at)

    aliases = {}
    if into is not None:
        in_specs.append(pl.BlockSpec(memory_space=pl.ANY))
        aliases = {len(args): 0}
        args.append(into)
    return call(
        functools.partial(down_kernel, counts),
        "down",
        (tiles,),
        in_specs,
        pl.BlockSpec((half_ff, TILE_D), place_out),
        jax.ShapeDtypeStruct((half_ff, width), BF16),
        [],
        4 * half_ff * TILE_D * slots * tiles,
        2 * (half_ff * TILE_D + 2 * slots * TILE_D) * tiles + 4 * slots * half_ff,
        aliases,
    )(*args)


def combine_kernel(experts, route_ref, prob_ref, slot_ref, *refs):
    out_ref = refs[-1]
    values = refs[0][...]
    for ref in refs[1:-1]:
        values += ref[...]
    capacity = values.shape[1]
    tokens = route_ref.shape[1]
    columns = values.T
    place = lax.broadcasted_iota(jnp.int32, (capacity, tokens), 0).astype(F32)
    route = route_ref[...]
    total = jnp.zeros(route.shape, F32)
    for e in range(experts):
        hit = slot_ref[e : e + 1, :] == place
        mine = jnp.sum(jnp.where(hit, columns[:, e : e + 1], 0.0), axis=0, keepdims=True)
        total = jnp.where(route == e, mine, total)
    out_ref[...] = total / prob_ref[...].astype(F32)


def combine(route, prob, slot, values):
    experts = values[0].shape[0]
    return pl.pallas_call(
        functools.partial(combine_kernel, experts),
        out_shape=jax.ShapeDtypeStruct(route.shape, F32),
        name="combine",
    )(route, prob, slot, *values)


def local(out_grad, route, gate_prob, w_down, gate_pre, up_pre):
    experts = lax.axis_size("expert")
    etp = lax.axis_size("etp")
    slots, ff = gate_pre.shape[1:]
    capacity = slots // experts
    width = out_grad.shape[1]
    where = jnp.stack(
        [lax.axis_index("etp") % 2, lax.axis_index("expert"), lax.axis_index("dp")]
    ).astype(jnp.int32)
    gate, up, w = gate_pre[0].T, up_pre[0].T, w_down[0]
    route, prob = route.T, gate_prob.T

    swap = [(2 * i, 2 * ((i - 1) % etp)) for i in range(etp)]
    swap += [(2 * i + 1, 2 * ((i + 1) % etp) + 1) for i in range(etp)]

    def fetch(send):
        x = send.reshape(experts, capacity, send.shape[1])
        x = lax.all_to_all(x, "expert", split_axis=0, concat_axis=0, tiled=True)
        return x.reshape(send.shape)

    def beside(x):
        return lax.ppermute(x, ("etp", "dp"), swap)

    def swap_dp(x):
        return lax.ppermute(x, "dp", [(0, 1), (1, 0)])

    c0, c1 = SHARED
    first, slot, pick = dispatch(where, route, prob, out_grad, experts, capacity)
    own0 = fetch(first)
    send1 = dispatch_more(where, pick, out_grad, c1, OWN)
    send2 = dispatch_more(where, pick, out_grad, DIRECT, SAME)
    act_other, act_mine = activation(where, gate, up)
    acts = (act_mine, swap_dp(act_other))
    own0, send1, send2, acts = lax.optimization_barrier((own0, send1, send2, acts))
    own1 = fetch(send1)
    oth0 = beside(own0)
    total = down(where, acts, [(own0, swap_dp(own0), c0, OWN)], width)
    own1, send2, total = lax.optimization_barrier((own1, send2, total))
    direct = fetch(send2)
    own1, oth0 = lax.optimization_barrier((own1, oth0))
    oth1 = beside(own1)
    raw = raw_part(where, w, [(own0, c0, OWN), (own1, c1, OWN), (oth0, c0, OTHER)])
    direct, oth1, raw = lax.optimization_barrier((direct, oth1, raw))
    late = [(oth1, c1, OTHER), (direct, DIRECT, SAME)]
    grad_gate, grad_up, sums = finish(where, gate, up, raw, w, late, experts)
    back = lax.all_to_all(sums, "expert", split_axis=0, concat_axis=0, tiled=True)
    pieces = [(own1, c1, OWN), (oth0, c0, OTHER)] + late
    pieces = [(rows, swap_dp(rows), chunk, side) for rows, chunk, side in pieces]
    total = down(where, acts, pieces, width, total)
    back, total = lax.optimization_barrier((back, total))
    others = [
        lax.ppermute(back, "etp", [(i, (i + k) % etp) for i in range(etp)]) for k in range(1, etp)
    ]
    grad_prob = combine(route, prob, slot, [back, *others])
    return grad_gate.T[None], grad_up.T[None], total[None], grad_prob.T


def solution(mesh):
    in_specs = (
        P(("expert", "dp"), None),
        P(("expert", "dp"), None),
        P(("expert", "dp"), None),
        P("expert", "etp", None),
        P("expert", "dp", "etp"),
        P("expert", "dp", "etp"),
    )
    out_specs = (
        P("expert", "dp", "etp"),
        P("expert", "dp", "etp"),
        P("expert", ("etp", "dp"), None),
        P(("expert", "dp"), None),
    )
    return jax.shard_map(local, mesh=mesh, in_specs=in_specs, out_specs=out_specs, check_vma=False)
```

time: 255 us -> 159 us (0.62)
  blocking collectives: 133 us -> 0 us
  Pallas kernels: 0 us -> 77.4 us
  matrix products: 47.3 us -> 0 us
  starting transfers between devices: 4.5 us -> 39.2 us
  other arithmetic: 26.1 us -> 0.61 us
  between operations: 14.2 us -> 0.77 us
  waiting for transfers between devices: 27.2 us -> 37.9 us
    all_to_all x2 -> x0, blocking collectives: 124 us -> none  [the longest x1 115 us: local(): lax.all_to_all(send_rows, 'expert', split_axis=0, concat_axis=0, tiled=True)]
    pallas_call x0 -> x9, Pallas kernels: none -> 77.4 us  [the longest x2 26.3 us: down(): call(functools.partial(down_kernel, counts), 'down', (tiles,), in_specs,...]
    dot_general x3 -> x0, matrix products: 47.3 us -> none  [the longest x1 23 us: local(): lax.dot_general(scaled, rows, (((0,), (0,)), ((), ())), preferred_element...]
    all_to_all x1 -> x4, waiting for transfers between devices: 6.26 us -> 32.9 us  [the longest x3 32.9 us: fetch(): x = lax.all_to_all(x, 'expert', split_axis=0, concat_axis=0, tiled=True)]
    reduce_scatter x1 -> x0, waiting for transfers between devices: 20.9 us -> none  [local(): lax.psum_scatter(lax.dot_general(scaled, rows, (((0,), (0,)), ((), ())),...]
    ppermute x0 -> x11, starting transfers between devices: none -> 17.8 us  [the longest x6 9.58 us: swap_dp(): return lax.ppermute(x, 'dp', [(0, 1), (1, 0)])]
    all_to_all x1 -> x4, starting transfers between devices: 4.46 us -> 21.4 us  [the longest x3 17.8 us: fetch(): x = lax.all_to_all(x, 'expert', split_axis=0, concat_axis=0, tiled=True)]
    broadcast_in_dim x2 -> x0, other arithmetic: 15.9 us -> none  [local(): return (grad_gate[None], grad_up[None], grad_down[None], grad_prob)]
  transfers between devices with their start and end apart: 2 -> 15, of which waited for: 2 -> 5; matrix products, arithmetic and copies ran while one was open for 4% -> 0% of each run, Pallas kernels for 0% -> 46%
where the time goes in v2:
time: 159 us; the launch traced here: 156 us
  Pallas kernels  77.4 us (49%)
  starting transfers between devices  39.2 us (25%)
  waiting for transfers between devices  37.9 us (24%)
    all_to_all x3, waiting for transfers between devices, fetch(): x = lax.all_to_all(x, 'expert', split_axis=0, concat_axis=0, tiled=True)  32.9 us
    pallas_call x2, Pallas kernels, down(): call(functools.partial(down_kernel, counts), 'down', (tiles,), in_specs,...  26.3 us
    all_to_all x3, starting transfers between devices, fetch(): x = lax.all_to_all(x, 'expert', split_axis=0, concat_axis=0, tiled=True)  17.8 us
    pallas_call x1, Pallas kernels, finish(): call(functools.partial(finish_kernel, len(pieces)), 'finish', (ff // TILE...  15.7 us
    pallas_call x1, Pallas kernels, raw_part(): call(functools.partial(raw_kernel, len(pieces), more), 'raw', (ff // TILE...  14.9 us
    ppermute x6, starting transfers between devices, swap_dp(): return lax.ppermute(x, 'dp', [(0, 1), (1, 0)])  9.58 us
    pallas_call x1, Pallas kernels, activation(): pl.pallas_call(act_kernel, out_shape=[out, out], grid_spec=pltpu.Prefetch...  7.9 us
    pallas_call x2, Pallas kernels, dispatch_more(): call(more_kernel, 'dispatch_more', (2,), [pl.BlockSpec((total // 2, token...  6.76 us
  transfers between devices with their start and end apart: 15, of which 5 were waited for; matrix products, arithmetic and copies ran while one was open for 0% of the time, Pallas kernels for 46%

profile of v2, /device:TPU:1, one launch (start us, length us, event | category | flops | bytes accessed | tf_op | source)
XLA Modules:
  0.0 156.5 jit_solution(4292954972312851290)
XLA Ops:
  0.6 0.6 pad_add_fusion.where_ref
  1.3 4.1 %dispatch.1 = (bf16[1536,768]{1,0:T(8,128)(2,1)}, f32[16,256]{1,0:T(8,128)}, bf16[1536,256]{1,0:T(8,128)(2,1)}) custom-call(s32[3]{0:T(128)} %pad_add_fusion.where_ref, s32[4,256]{1,0:T(4,128)} %bitcast.54, bf16[4,256]{1,0:T(4,128)(2,1)} %bitcast.56, bf16[256,3072]{1,0:T(8,128)(2,1)} %grad_ref.5), custom_call_target="tpu_custom_call" | custom-call | flops 150994944 | bytes 589824 | tf_op jit(solution)/shard_map/dispatch/pallas_call | solution.py:97
  5.3 8.6 %all-to-all-start = ((bf16[16,96,768]{2,1,0:T(8,128)(2,1)}), bf16[16,96,768]{2,1,0:T(8,128)(2,1)S(1)}, u32[]{:S(2)}, u32[]{:S(2)}) async-start(bf16[16,96,768]{2,1,0:T(8,128)(2,1)} %bitcast.49), calls=%async_computation | async-start | bytes 4718592 | tf_op jit(solution)/shard_map/all_to_all | solution.py:404
  13.9 7.9 %activation.1 = (bf16[672,1536]{1,0:T(8,128)(2,1)}, bf16[672,1536]{1,0:T(8,128)(2,1)}) custom-call(s32[3]{0:T(128)} %pad_add_fusion.where_ref, bf16[1344,1536]{1,0:T(8,128)(2,1)} %bitcast.39, bf16[1344,1536]{1,0:T(8,128)(2,1)} %bitcast.41), custom_call_target="tpu_custom_call" | custom-call | flops 10321920 | bytes 3096576 | tf_op jit(solution)/shard_map/activation/pallas_call | solution.py:182
  21.8 1.0 collective-permute-start
  22.8 3.4 %dispatch_more.3 = bf16[1536,512]{1,0:T(8,128)(2,1)} custom-call(s32[3]{0:T(128)} %pad_add_fusion.where_ref, bf16[1536,256]{1,0:T(8,128)(2,1)} %get-tuple-element.28.pick_ref, bf16[256,3072]{1,0:T(8,128)(2,1)} %grad_ref.5), custom_call_target="tpu_custom_call" | custom-call | flops 100663296 | bytes 393216 | tf_op jit(solution)/shard_map/dispatch_more/pallas_call | solution.py:132
  26.2 3.4 %dispatch_more.2 = bf16[1536,512]{1,0:T(8,128)(2,1)} custom-call(s32[3]{0:T(128)} %pad_add_fusion.where_ref, bf16[1536,256]{1,0:T(8,128)(2,1)} %get-tuple-element.28.pick_ref, bf16[256,3072]{1,0:T(8,128)(2,1)} %grad_ref.5), custom_call_target="tpu_custom_call" | custom-call | flops 100663296 | bytes 393216 | tf_op jit(solution)/shard_map/dispatch_more/pallas_call | solution.py:132
  29.6 16.1 %all-to-all-done = bf16[16,96,768]{2,1,0:T(8,128)(2,1)S(1)} async-done(((bf16[16,96,768]{2,1,0:T(8,128)(2,1)}), bf16[16,96,768]{2,1,0:T(8,128)(2,1)S(1)}, u32[]{:S(2)}, u32[]{:S(2)}) %all-to-all-start) | async-done | bytes 2359328 | tf_op jit(solution)/shard_map/all_to_all | solution.py:404
  45.6 2.9 %collective-permute-start.1 = (bf16[1536,768]{1,0:T(8,128)(2,1)S(1)}, bf16[1536,768]{1,0:T(8,128)(2,1)}, u32[]{:S(2)}, u32[]{:S(2)}) collective-permute-start(bf16[1536,768]{1,0:T(8,128)(2,1)S(1)} %bitcast.35), channel_id=1, source_target_pairs={{0,1},{1,0},{2,3},{3,2},{4,5},{5,4},{6,7},{7,6},{8,9},{9,8},{10,11... | collective-permute-start | bytes 7077896 | tf_op jit(solution)/shard_map/ppermute | solution.py:411
  48.6 1.2 collective-permute-start.2
  49.8 4.4 %all-to-all-start.1 = ((bf16[16,96,512]{2,1,0:T(8,128)(2,1)}), bf16[16,96,512]{2,1,0:T(8,128)(2,1)}, u32[]{:S(2)}, u32[]{:S(2)}) async-start(bf16[16,96,512]{2,1,0:T(8,128)(2,1)} %bitcast.48), calls=%async_computation.1 | async-start | bytes 3145728 | tf_op jit(solution)/shard_map/all_to_all | solution.py:404
  54.2 0.0 collective-permute-done.1.refs_1_
  54.2 8.1 %down.2.refs_8_ = bf16[672,3072]{1,0:T(8,128)(2,1)} custom-call(s32[3]{0:T(128)} %pad_add_fusion.where_ref, bf16[672,1536]{1,0:T(8,128)(2,1)} %get-tuple-element.33.here_ref, bf16[672,1536]{1,0:T(8,128)(2,1)} %collective-permute-done.there_ref, bf16[1536,768]{1,0:T(8,128)(2,1)} %bitcast.37, bf16[1536,768]{1,0:T(8,128)(2,1)} %collective-permute-done.1.refs_1_), custom_call_target="tpu_custom_call" | custom-call | flops 792723456 | bytes 2469888 | tf_op jit(solution)/shard_map/down/pallas_call | solution.py:346
  62.4 12.5 %all-to-all-done.1 = bf16[16,96,512]{2,1,0:T(8,128)(2,1)} async-done(((bf16[16,96,512]{2,1,0:T(8,128)(2,1)}), bf16[16,96,512]{2,1,0:T(8,128)(2,1)}, u32[]{:S(2)}, u32[]{:S(2)}) %all-to-all-start.1) | async-done | bytes 1572896 | tf_op jit(solution)/shard_map/all_to_all | solution.py:404
  74.8 2.7 %collective-permute-done.2.refs_4_.refs_2_ = bf16[1536,768]{1,0:T(8,128)(2,1)} collective-permute-done((bf16[1536,768]{1,0:T(8,128)(2,1)S(1)}, bf16[1536,768]{1,0:T(8,128)(2,1)}, u32[]{:S(2)}, u32[]{:S(2)}) %collective-permute-start.2) | collective-permute-done | bytes 2359328 | tf_op jit(solution)/shard_map/ppermute | solution.py:408
  77.6 1.8 %collective-permute-start.3 = (bf16[1536,512]{1,0:T(8,128)(2,1)}, bf16[1536,512]{1,0:T(8,128)(2,1)S(1)}, u32[]{:S(2)}, u32[]{:S(2)}) collective-permute-start(bf16[1536,512]{1,0:T(8,128)(2,1)} %bitcast.14.refs_2_.refs_0_), channel_id=1, source_target_pairs={{0,6},{2,0},{4,2},{6,4},{1,3},{3,5},{5,7},{7,1},{8,14},{10,8},{12,... | collective-permute-start | bytes 4718600 | tf_op jit(solution)/shard_map/ppermute | solution.py:408
  79.3 4.8 %all-to-all-start.2 = ((bf16[16,96,512]{2,1,0:T(8,128)(2,1)}), bf16[16,96,512]{2,1,0:T(8,128)(2,1)S(1)}, u32[]{:S(2)}, u32[]{:S(2)}) async-start(bf16[16,96,512]{2,1,0:T(8,128)(2,1)} %bitcast.47), calls=%async_computation.2 | async-start | bytes 3145728 | tf_op jit(solution)/shard_map/all_to_all | solution.py:404
  84.1 1.2 collective-permute-start.5
  85.3 0.1 collective-permute-start.4
  85.4 14.9 %raw.1.before_ref = f32[1344,1536]{1,0:T(8,128)} custom-call(s32[3]{0:T(128)} %pad_add_fusion.where_ref, bf16[1536,768]{1,0:T(8,128)(2,1)} %bitcast.38, bf16[1344,3072]{1,0:T(8,128)(2,1)} %bitcast.30, bf16[1536,512]{1,0:T(8,128)(2,1)} %bitcast.14.refs_2_.refs_0_, bf16[1344,3072]{1,0:T(8,128)(2,1)} %bitcast.31, ...), custom_call_target="tpu_custom_call" | custom-call | flops 2113929216 | bytes 7077888 | tf_op jit(solution)/shard_map/raw/pallas_call | solution.py:235
  100.2 4.3 %all-to-all-done.2 = bf16[16,96,512]{2,1,0:T(8,128)(2,1)S(1)} async-done(((bf16[16,96,512]{2,1,0:T(8,128)(2,1)}), bf16[16,96,512]{2,1,0:T(8,128)(2,1)S(1)}, u32[]{:S(2)}, u32[]{:S(2)}) %all-to-all-start.2) | async-done | bytes 1572896 | tf_op jit(solution)/shard_map/all_to_all | solution.py:404
  104.6 4.3 %collective-permute-start.6 = (bf16[1536,512]{1,0:T(8,128)(2,1)S(1)}, bf16[1536,512]{1,0:T(8,128)(2,1)}, u32[]{:S(2)}, u32[]{:S(2)}) collective-permute-start(bf16[1536,512]{1,0:T(8,128)(2,1)S(1)} %collective-permute-done.3.refs_0_.refs_4_), channel_id=1, source_target_pairs={{0,1},{1,0},{2,3},{3,2},{4,5},{5,4},{6,7},{7,6},{8,9},{9,8},{10,11... | collective-permute-start | bytes 4718600 | tf_op jit(solution)/shard_map/ppermute | solution.py:411
  108.9 0.1 collective-permute-start.7
  109.0 15.7 %finish.1 = (bf16[1344,1536]{1,0:T(8,128)(2,1)}, bf16[1344,1536]{1,0:T(8,128)(2,1)}, f32[16,96]{1,0:T(8,128)}) custom-call(s32[3]{0:T(128)} %pad_add_fusion.where_ref, bf16[1344,1536]{1,0:T(8,128)(2,1)} %bitcast.40, bf16[1344,1536]{1,0:T(8,128)(2,1)} %bitcast.42, f32[1344,1536]{1,0:T(8,128)} %raw.1.before_ref, bf16[1536,512]{1,0:T(8,128)(2,1)} %copy-done.2, ...), custom_call_target="tpu_custom_call" | custom-call | flops 1056964608 | bytes 7667712 | tf_op jit(solution)/shard_map/finish/pallas_call | solution.py:290
  124.7 3.6 %all-to-all-start.3 = ((f32[16,1,96]{2,1,0:T(1,128)}), f32[16,1,96]{2,1,0:T(1,128)S(1)}, u32[]{:S(2)}, u32[]{:S(2)}) async-start(f32[16,1,96]{2,1,0:T(1,128)} %bitcast.58), calls=%async_computation.3 | async-start | bytes 16384 | tf_op jit(solution)/shard_map/all_to_all | solution.py:432
  128.4 18.1 %down.3 = bf16[672,3072]{1,0:T(8,128)(2,1)} custom-call(s32[3]{0:T(128)} %pad_add_fusion.where_ref, bf16[672,1536]{1,0:T(8,128)(2,1)} %get-tuple-element.33.here_ref, bf16[672,1536]{1,0:T(8,128)(2,1)} %collective-permute-done.there_ref, bf16[1536,512]{1,0:T(8,128)(2,1)} %bitcast.14.refs_2_.refs_0_, ...), custom_call_target="tpu_custom_call", output_to_operand_aliasing={{}: (11, {})} | custom-call | flops 2378170368 | bytes 5345280 | tf_op jit(solution)/shard_map/down/pallas_call | solution.py:346
  146.5 0.1 collective-permute-start.10
  146.6 3.4 %collective-permute-start.8 = (f32[16,96]{1,0:T(8,128)S(1)}, f32[16,96]{1,0:T(8,128)S(1)}, u32[]{:S(2)}, u32[]{:S(2)}) collective-permute-start(f32[16,96]{1,0:T(8,128)S(1)} %bitcast.51), channel_id=1, source_target_pairs={{0,2},{2,4},{4,6},{6,0},{1,3},{3,5},{5,7},{7,1},{8,10},{10,12},{12... | collective-permute-start | bytes 18440 | tf_op jit(solution)/shard_map/ppermute | solution.py:438
  150.0 1.7 %collective-permute-start.9 = (f32[16,96]{1,0:T(8,128)S(1)}, f32[16,96]{1,0:T(8,128)S(1)}, u32[]{:S(2)}, u32[]{:S(2)}) collective-permute-start(f32[16,96]{1,0:T(8,128)S(1)} %bitcast.52), channel_id=1, source_target_pairs={{0,4},{2,6},{4,0},{6,2},{1,5},{3,7},{5,1},{7,3},{8,12},{10,14},{12... | collective-permute-start | bytes 18440 | tf_op jit(solution)/shard_map/ppermute | solution.py:438
  151.8 2.3 %collective-permute-done.9.refs_2_ = f32[16,96]{1,0:T(8,128)S(1)} collective-permute-done((f32[16,96]{1,0:T(8,128)S(1)}, f32[16,96]{1,0:T(8,128)S(1)}, u32[]{:S(2)}, u32[]{:S(2)}) %collective-permute-start.9) | collective-permute-done | bytes 6176 | tf_op jit(solution)/shard_map/ppermute | solution.py:438
  154.1 0.6 copy-done.6
  154.7 1.8 %combine.1 = f32[4,256]{1,0:T(4,128)} custom-call(s32[4,256]{1,0:T(4,128)} %bitcast.55, bf16[4,256]{1,0:T(4,128)(2,1)} %bitcast.57, f32[16,256]{1,0:T(8,128)} %get-tuple-element.48.slot_ref, f32[16,96]{1,0:T(8,128)} %bitcast.53, f32[16,96]{1,0:T(8,128)} %copy-done.5, f32[16,96]{1,0:T(8,128)} %copy-done.6, f32[16,96]{1,0:T(8,128)} %copy-done.4), custom_call_target="tpu_custom_call" | custom-call | tf_op jit(solution)/shard_map/combine/pallas_call | solution.py:380
  (22 shorter events, 0.0 us)
Async XLA Ops:
  5.3 40.3 %all-to-all-start = ((bf16[16,96,768]{2,1,0:T(8,128)(2,1)}), bf16[16,96,768]{2,1,0:T(8,128)(2,1)S(1)}, u32[]{:S(2)}, u32[]{:S(2)}) async-start(bf16[16,96,768]{2,1,0:T(8,128)(2,1)} %bitcast.49), calls=%async_computation | async-start | bytes 4718592 | tf_op jit(solution)/shard_map/all_to_all | solution.py:404
  21.8 7.7 %collective-permute-start = (bf16[672,1536]{1,0:T(8,128)(2,1)}, bf16[672,1536]{1,0:T(8,128)(2,1)}, u32[]{:S(2)}, u32[]{:S(2)}) collective-permute-start(bf16[672,1536]{1,0:T(8,128)(2,1)} %get-tuple-element.30), channel_id=1, source_target_pairs={{0,1},{1,0},{2,3},{3,2},{4,5},{5,4},{6,7},{7,6},{8,9},{9,8},{10,11... | collective-permute-start | bytes 6193160 | tf_op jit(solution)/shard_map/ppermute | solution.py:411
  45.6 8.6 %copy-start = (bf16[16,96,768]{2,1,0:T(8,128)(2,1)}, bf16[16,96,768]{2,1,0:T(8,128)(2,1)S(1)}, u32[]{:S(2)}) copy-start(bf16[16,96,768]{2,1,0:T(8,128)(2,1)S(1)} %all-to-all-done) | copy-start | bytes 7077892
  45.6 8.6 %collective-permute-start.1 = (bf16[1536,768]{1,0:T(8,128)(2,1)S(1)}, bf16[1536,768]{1,0:T(8,128)(2,1)}, u32[]{:S(2)}, u32[]{:S(2)}) collective-permute-start(bf16[1536,768]{1,0:T(8,128)(2,1)S(1)} %bitcast.35), channel_id=1, source_target_pairs={{0,1},{1,0},{2,3},{3,2},{4,5},{5,4},{6,7},{7,6},{8,9},{9,8},{10,11... | collective-permute-start | bytes 7077896 | tf_op jit(solution)/shard_map/ppermute | solution.py:411
  48.6 29.0 %collective-permute-start.2 = (bf16[1536,768]{1,0:T(8,128)(2,1)S(1)}, bf16[1536,768]{1,0:T(8,128)(2,1)}, u32[]{:S(2)}, u32[]{:S(2)}) collective-permute-start(bf16[1536,768]{1,0:T(8,128)(2,1)S(1)} %bitcast.36), channel_id=1, source_target_pairs={{0,6},{2,0},{4,2},{6,4},{1,3},{3,5},{5,7},{7,1},{8,14},{10,8},{12,... | collective-permute-start | bytes 7077896 | tf_op jit(solution)/shard_map/ppermute | solution.py:408
  49.8 25.1 %all-to-all-start.1 = ((bf16[16,96,512]{2,1,0:T(8,128)(2,1)}), bf16[16,96,512]{2,1,0:T(8,128)(2,1)}, u32[]{:S(2)}, u32[]{:S(2)}) async-start(bf16[16,96,512]{2,1,0:T(8,128)(2,1)} %bitcast.48), calls=%async_computation.1 | async-start | bytes 3145728 | tf_op jit(solution)/shard_map/all_to_all | solution.py:404
  77.6 27.0 %collective-permute-start.3 = (bf16[1536,512]{1,0:T(8,128)(2,1)}, bf16[1536,512]{1,0:T(8,128)(2,1)S(1)}, u32[]{:S(2)}, u32[]{:S(2)}) collective-permute-start(bf16[1536,512]{1,0:T(8,128)(2,1)} %bitcast.14.refs_2_.refs_0_), channel_id=1, source_target_pairs={{0,6},{2,0},{4,2},{6,4},{1,3},{3,5},{5,7},{7,1},{8,14},{10,8},{12,... | collective-permute-start | bytes 4718600 | tf_op jit(solution)/shard_map/ppermute | solution.py:408
  79.3 25.2 %all-to-all-start.2 = ((bf16[16,96,512]{2,1,0:T(8,128)(2,1)}), bf16[16,96,512]{2,1,0:T(8,128)(2,1)S(1)}, u32[]{:S(2)}, u32[]{:S(2)}) async-start(bf16[16,96,512]{2,1,0:T(8,128)(2,1)} %bitcast.47), calls=%async_computation.2 | async-start | bytes 3145728 | tf_op jit(solution)/shard_map/all_to_all | solution.py:404
  84.1 44.2 %collective-permute-start.5 = (bf16[1536,768]{1,0:T(8,128)(2,1)}, bf16[1536,768]{1,0:T(8,128)(2,1)}, u32[]{:S(2)}, u32[]{:S(2)}) collective-permute-start(bf16[1536,768]{1,0:T(8,128)(2,1)} %collective-permute-done.2.refs_4_.refs_2_), channel_id=1, source_target_pairs={{0,1},{1,0},{2,3},{3,2},{4,5},{5,4},{6,7},{7,6},{8,9},{9,8},{10,11... | collective-permute-start | bytes 7077896 | tf_op jit(solution)/shard_map/ppermute | solution.py:411
  85.3 43.1 %collective-permute-start.4 = (bf16[1536,512]{1,0:T(8,128)(2,1)}, bf16[1536,512]{1,0:T(8,128)(2,1)}, u32[]{:S(2)}, u32[]{:S(2)}) collective-permute-start(bf16[1536,512]{1,0:T(8,128)(2,1)} %bitcast.14.refs_2_.refs_0_), channel_id=1, source_target_pairs={{0,1},{1,0},{2,3},{3,2},{4,5},{5,4},{6,7},{7,6},{8,9},{9,8},{10,11... | collective-permute-start | bytes 4718600 | tf_op jit(solution)/shard_map/ppermute | solution.py:411
  104.6 4.4 %copy-start.1 = (bf16[16,96,512]{2,1,0:T(8,128)(2,1)}, bf16[16,96,512]{2,1,0:T(8,128)(2,1)S(1)}, u32[]{:S(2)}) copy-start(bf16[16,96,512]{2,1,0:T(8,128)(2,1)S(1)} %all-to-all-done.2) | copy-start | bytes 4718596
  104.6 4.4 %copy-start.2 = (bf16[1536,512]{1,0:T(8,128)(2,1)}, bf16[1536,512]{1,0:T(8,128)(2,1)S(1)}, u32[]{:S(2)}) copy-start(bf16[1536,512]{1,0:T(8,128)(2,1)S(1)} %collective-permute-done.3.refs_0_.refs_4_) | copy-start | bytes 4718596
  104.6 23.8 %collective-permute-start.6 = (bf16[1536,512]{1,0:T(8,128)(2,1)S(1)}, bf16[1536,512]{1,0:T(8,128)(2,1)}, u32[]{:S(2)}, u32[]{:S(2)}) collective-permute-start(bf16[1536,512]{1,0:T(8,128)(2,1)S(1)} %collective-permute-done.3.refs_0_.refs_4_), channel_id=1, source_target_pairs={{0,1},{1,0},{2,3},{3,2},{4,5},{5,4},{6,7},{7,6},{8,9},{9,8},{10,11... | collective-permute-start | bytes 4718600 | tf_op jit(solution)/shard_map/ppermute | solution.py:411
  108.9 19.5 %collective-permute-start.7 = (bf16[1536,512]{1,0:T(8,128)(2,1)S(1)}, bf16[1536,512]{1,0:T(8,128)(2,1)}, u32[]{:S(2)}, u32[]{:S(2)}) collective-permute-start(bf16[1536,512]{1,0:T(8,128)(2,1)S(1)} %bitcast.44), channel_id=1, source_target_pairs={{0,1},{1,0},{2,3},{3,2},{4,5},{5,4},{6,7},{7,6},{8,9},{9,8},{10,11... | collective-permute-start | bytes 4718600 | tf_op jit(solution)/shard_map/ppermute | solution.py:411
  124.7 21.8 %all-to-all-start.3 = ((f32[16,1,96]{2,1,0:T(1,128)}), f32[16,1,96]{2,1,0:T(1,128)S(1)}, u32[]{:S(2)}, u32[]{:S(2)}) async-start(f32[16,1,96]{2,1,0:T(1,128)} %bitcast.58), calls=%async_computation.3 | async-start | bytes 16384 | tf_op jit(solution)/shard_map/all_to_all | solution.py:432
  146.5 7.5 %copy-start.3 = (f32[16,1,96]{2,1,0:T(1,128)}, f32[16,1,96]{2,1,0:T(1,128)S(1)}, u32[]{:S(2)}) copy-start(f32[16,1,96]{2,1,0:T(1,128)S(1)} %all-to-all-done.3) | copy-start | bytes 18436
  146.5 5.2 %collective-permute-start.10 = (f32[16,96]{1,0:T(8,128)S(1)}, f32[16,96]{1,0:T(8,128)S(1)}, u32[]{:S(2)}, u32[]{:S(2)}) collective-permute-start(f32[16,96]{1,0:T(8,128)S(1)} %bitcast.50), channel_id=1, source_target_pairs={{0,6},{2,0},{4,2},{6,4},{1,7},{3,1},{5,3},{7,5},{8,14},{10,8},{12,... | collective-permute-start | bytes 18440 | tf_op jit(solution)/shard_map/ppermute | solution.py:438
  146.6 5.1 %collective-permute-start.8 = (f32[16,96]{1,0:T(8,128)S(1)}, f32[16,96]{1,0:T(8,128)S(1)}, u32[]{:S(2)}, u32[]{:S(2)}) collective-permute-start(f32[16,96]{1,0:T(8,128)S(1)} %bitcast.51), channel_id=1, source_target_pairs={{0,2},{2,4},{4,6},{6,0},{1,3},{3,5},{5,7},{7,1},{8,10},{10,12},{12... | collective-permute-start | bytes 18440 | tf_op jit(solution)/shard_map/ppermute | solution.py:438
  150.0 4.0 %collective-permute-start.9 = (f32[16,96]{1,0:T(8,128)S(1)}, f32[16,96]{1,0:T(8,128)S(1)}, u32[]{:S(2)}, u32[]{:S(2)}) collective-permute-start(f32[16,96]{1,0:T(8,128)S(1)} %bitcast.52), channel_id=1, source_target_pairs={{0,4},{2,6},{4,0},{6,2},{1,5},{3,7},{5,1},{7,3},{8,12},{10,14},{12... | collective-permute-start | bytes 18440 | tf_op jit(solution)/shard_map/ppermute | solution.py:438
  151.8 2.3 %copy-start.4 = (f32[16,96]{1,0:T(8,128)}, f32[16,96]{1,0:T(8,128)S(1)}, u32[]{:S(2)}) copy-start(f32[16,96]{1,0:T(8,128)S(1)} %collective-permute-done.10.refs_3_) | copy-start | bytes 18436
  151.8 2.3 %copy-start.5 = (f32[16,96]{1,0:T(8,128)}, f32[16,96]{1,0:T(8,128)S(1)}, u32[]{:S(2)}) copy-start(f32[16,96]{1,0:T(8,128)S(1)} %collective-permute-done.8.refs_1_) | copy-start | bytes 18436
  154.1 0.6 copy-start.6

commit v3 on v2

--- a/solution.py
+++ b/solution.py
@@ -10,19 +10,19 @@
 BF16 = jnp.bfloat16
 F32 = jnp.float32
 LANES = 128
-SHARED = ((0, 768), (1536, 512))
-DIRECT = (2560, 512)
+SHARED = ((0, 512), (1536, 768))
+DIRECT = (1024, 512)
 TILE_FF = 336
 TILE_D = 256
 SUB = 16
 COLS = 256
-VMEM_MB = 56
+VMEM_MB = {"dispatch": 16, "dispatch_more": 12, "activation": 16, "raw": 56, "finish": 56, "down": 20}
 NT = (((1,), (1,)), ((), ()))
 
 
-def params():
+def params(name):
     return pltpu.CompilerParams(
-        dimension_semantics=("arbitrary",), vmem_limit_bytes=VMEM_MB << 20
+        dimension_semantics=("arbitrary",), vmem_limit_bytes=VMEM_MB[name] << 20
     )
 
 
@@ -43,7 +43,7 @@
             scratch_shapes=scratch,
         ),
         input_output_aliases=aliases or {},
-        compiler_params=params(),
+        compiler_params=params(name),
         cost_estimate=cost(flops, moved),
         name=name,
     )
@@ -140,8 +140,8 @@
         pl.BlockSpec((total // 2, part), lambda i, s: (i, 0)),
         jax.ShapeDtypeStruct((total, part), BF16),
         [],
-        2 * total * tokens * part,
-        2 * total * part,
+        4,
+        4,
     )(where, pick, grad)
 
 
@@ -192,9 +192,9 @@
             ],
         ),
         compiler_params=pltpu.CompilerParams(
-            dimension_semantics=("arbitrary", "arbitrary"), vmem_limit_bytes=VMEM_MB << 20
+            dimension_semantics=("arbitrary", "arbitrary"), vmem_limit_bytes=VMEM_MB["activation"] << 20
         ),
-        cost_estimate=cost(20 * ff * slots, 6 * ff * slots),
+        cost_estimate=cost(4, 4),
         name="activation",
     )(where, gate, up)
 
@@ -412,31 +412,37 @@
 
     c0, c1 = SHARED
     first, slot, pick = dispatch(where, route, prob, out_grad, experts, capacity)
+    gate, up, pick = lax.optimization_barrier((gate, up, pick))
     own0 = fetch(first)
     send1 = dispatch_more(where, pick, out_grad, c1, OWN)
     send2 = dispatch_more(where, pick, out_grad, DIRECT, SAME)
     act_other, act_mine = activation(where, gate, up)
+    own0, send1, send2, act_other, act_mine = lax.optimization_barrier(
+        (own0, send1, send2, act_other, act_mine)
+    )
     acts = (act_mine, swap_dp(act_other))
-    own0, send1, send2, acts = lax.optimization_barrier((own0, send1, send2, acts))
     own1 = fetch(send1)
     oth0 = beside(own0)
     total = down(where, acts, [(own0, swap_dp(own0), c0, OWN)], width)
+    total = down(where, acts, [(oth0, swap_dp(oth0), c0, OTHER)], width, total)
     own1, send2, total = lax.optimization_barrier((own1, send2, total))
     direct = fetch(send2)
-    own1, oth0 = lax.optimization_barrier((own1, oth0))
     oth1 = beside(own1)
     raw = raw_part(where, w, [(own0, c0, OWN), (own1, c1, OWN), (oth0, c0, OTHER)])
-    direct, oth1, raw = lax.optimization_barrier((direct, oth1, raw))
+    pieces = [(own1, swap_dp(own1), c1, OWN)]
+    total = down(where, acts, pieces, width, total)
+    direct, oth1, raw, total = lax.optimization_barrier((direct, oth1, raw, total))
     late = [(oth1, c1, OTHER), (direct, DIRECT, SAME)]
     grad_gate, grad_up, sums = finish(where, gate, up, raw, w, late, experts)
     back = lax.all_to_all(sums, "expert", split_axis=0, concat_axis=0, tiled=True)
-    pieces = [(own1, c1, OWN), (oth0, c0, OTHER)] + late
-    pieces = [(rows, swap_dp(rows), chunk, side) for rows, chunk, side in pieces]
-    total = down(where, acts, pieces, width, total)
+    pieces = [(rows, swap_dp(rows), chunk, side) for rows, chunk, side in late]
+    total = down(where, acts, pieces[:1], width, total)
     back, total = lax.optimization_barrier((back, total))
     others = [
         lax.ppermute(back, "etp", [(i, (i + k) % etp) for i in range(etp)]) for k in range(1, etp)
     ]
+    total = down(where, acts, pieces[1:], width, total)
+    others, total = lax.optimization_barrier((others, total))
     grad_prob = combine(route, prob, slot, [back, *others])
     return grad_gate.T[None], grad_up.T[None], total[None], grad_prob.T
 

time: 159 us -> 149 us (0.937)
  waiting for transfers between devices: 37.9 us -> 23.2 us
  local copies, waits for them, and re-layouts: 0.6 us -> 11.6 us
  Pallas kernels: 77.4 us -> 68.5 us
  starting transfers between devices: 39.2 us -> 43.4 us
    all_to_all x3, waiting for transfers between devices: 32.9 us -> 10.3 us  [fetch(): x = lax.all_to_all(x, 'expert', split_axis=0, concat_axis=0, tiled=True)]
    unnamed x14 -> x44, local copies, waits for them, and re-layouts: 0.6 us -> 11.6 us
    ppermute x2, waiting for transfers between devices: 2.73 us -> 12.8 us  [beside(): return lax.ppermute(x, ('etp', 'dp'), swap)]
    ppermute x6, starting transfers between devices: 9.58 us -> 15.4 us  [swap_dp(): return lax.ppermute(x, 'dp', [(0, 1), (1, 0)])]
    pallas_call x1, Pallas kernels: 7.9 us -> 3.8 us  [activation(): pl.pallas_call(act_kernel, out_shape=[out, out], grid_spec=pltpu.Prefetch...]
    pallas_call x2, Pallas kernels: 6.76 us -> 2.89 us  [dispatch_more(): call(more_kernel, 'dispatch_more', (2,), [pl.BlockSpec((total // 2, token...]
    pallas_call x1, Pallas kernels: 4.07 us -> 1.27 us  [dispatch(): call(functools.partial(dispatch_kernel, experts, capacity), 'dispatch', (...]
    ppermute x3, starting transfers between devices: 5.21 us -> 2.79 us  [local(): lax.ppermute(back, 'etp', [(i, (i + k) % etp) for i in range(etp)])]
  transfers between devices with their start and end apart: 15 -> 15, of which waited for: 5 -> 4; matrix products, arithmetic and copies ran while one was open for 0% -> 0% of each run, Pallas kernels for 46% -> 44%
where the time goes in v3:
time: 149 us; the launch traced here: 148 us
  Pallas kernels  68.5 us (46%)
  starting transfers between devices  43.4 us (29%)
  waiting for transfers between devices  23.2 us (16%)
  local copies, waits for them, and re-layouts  11.6 us (8%)
    pallas_call x5, Pallas kernels, down(): call(functools.partial(down_kernel, counts), 'down', (tiles,), in_specs,...  28.5 us
    all_to_all x3, starting transfers between devices, fetch(): x = lax.all_to_all(x, 'expert', split_axis=0, concat_axis=0, tiled=True)  18.4 us
    pallas_call x1, Pallas kernels, finish(): call(functools.partial(finish_kernel, len(pieces)), 'finish', (ff // TILE...  16.4 us
    ppermute x6, starting transfers between devices, swap_dp(): return lax.ppermute(x, 'dp', [(0, 1), (1, 0)])  15.4 us
    pallas_call x1, Pallas kernels, raw_part(): call(functools.partial(raw_kernel, len(pieces), more), 'raw', (ff // TILE...  13.7 us
    ppermute x2, waiting for transfers between devices, beside(): return lax.ppermute(x, ('etp', 'dp'), swap)  12.8 us
    unnamed x44, local copies, waits for them, and re-layouts  11.6 us
    all_to_all x3, waiting for transfers between devices, fetch(): x = lax.all_to_all(x, 'expert', split_axis=0, concat_axis=0, tiled=True)  10.3 us
  transfers between devices with their start and end apart: 15, of which 4 were waited for; matrix products, arithmetic and copies ran while one was open for 0% of the time, Pallas kernels for 44%

profile of v3, /device:TPU:1, one launch (start us, length us, event | category | flops | bytes accessed | tf_op | source)
XLA Modules:
  0.0 147.5 jit_solution(9254717604498306737)
XLA Ops:
  0.7 1.4 copy-done.6
  3.5 1.3 dispatch.1
  4.8 1.1 copy-done.10
  5.9 8.6 %all-to-all-start = ((bf16[16,96,512]{2,1,0:T(8,128)(2,1)}), bf16[16,96,512]{2,1,0:T(8,128)(2,1)}, u32[]{:S(2)}, u32[]{:S(2)}) async-start(bf16[16,96,512]{2,1,0:T(8,128)(2,1)} %bitcast.36), calls=%async_computation | async-start | bytes 3145728 | tf_op jit(solution)/shard_map/all_to_all | solution.py:404
  14.6 1.3 dispatch_more.3
  16.0 1.2 copy-done.9
  17.1 1.6 %dispatch_more.2 = bf16[1536,768]{1,0:T(8,128)(2,1)S(1)} custom-call(s32[3]{0:T(128)S(1)} %pad_add_fusion.where_ref, bf16[1536,256]{1,0:T(8,128)(2,1)S(1)} %get-tuple-element.37.pick_ref, bf16[256,3072]{1,0:T(8,128)(2,1)S(1)} %copy-done.7), custom_call_target="tpu_custom_call" | custom-call | flops 1 | bytes 1 | tf_op jit(solution)/shard_map/dispatch_more/pallas_call | solution.py:132
  18.7 1.4 copy-done.8
  20.1 3.8 %activation.1 = (bf16[672,1536]{1,0:T(8,128)(2,1)S(1)}, bf16[672,1536]{1,0:T(8,128)(2,1)S(1)}) custom-call(s32[3]{0:T(128)S(1)} %pad_add_fusion.where_ref, bf16[1344,1536]{1,0:T(8,128)(2,1)S(1)} %bitcast.31, bf16[1344,1536]{1,0:T(8,128)(2,1)S(1)} %bitcast.33), custom_call_target="tpu_custom_call" | custom-call | flops 1 | bytes 1 | tf_op jit(solution)/shard_map/activation/pallas_call | solution.py:182
  23.9 1.3 copy-done.17
  25.2 10.0 %all-to-all-done = bf16[16,96,512]{2,1,0:T(8,128)(2,1)} async-done(((bf16[16,96,512]{2,1,0:T(8,128)(2,1)}), bf16[16,96,512]{2,1,0:T(8,128)(2,1)}, u32[]{:S(2)}, u32[]{:S(2)}) %all-to-all-start) | async-done | bytes 1572896 | tf_op jit(solution)/shard_map/all_to_all | solution.py:404
  35.3 1.2 collective-permute-start.1
  36.5 5.4 %all-to-all-start.1 = ((bf16[16,96,768]{2,1,0:T(8,128)(2,1)}), bf16[16,96,768]{2,1,0:T(8,128)(2,1)}, u32[]{:S(2)}, u32[]{:S(2)}) async-start(bf16[16,96,768]{2,1,0:T(8,128)(2,1)} %bitcast.34), calls=%async_computation.1 | async-start | bytes 4718592 | tf_op jit(solution)/shard_map/all_to_all | solution.py:404
  41.9 4.8 %collective-permute-start = (bf16[672,1536]{1,0:T(8,128)(2,1)}, bf16[672,1536]{1,0:T(8,128)(2,1)S(1)}, u32[]{:S(2)}, u32[]{:S(2)}) collective-permute-start(bf16[672,1536]{1,0:T(8,128)(2,1)} %copy-done.17), channel_id=1, source_target_pairs={{0,1},{1,0},{2,3},{3,2},{4,5},{5,4},{6,7},{7,6},{8,9},{9,8},{10,11... | collective-permute-start | bytes 6193160 | tf_op jit(solution)/shard_map/ppermute | solution.py:411
  46.8 9.6 %collective-permute-done.1.refs_0_.refs_4_ = bf16[1536,512]{1,0:T(8,128)(2,1)} collective-permute-done((bf16[1536,512]{1,0:T(8,128)(2,1)}, bf16[1536,512]{1,0:T(8,128)(2,1)}, u32[]{:S(2)}, u32[]{:S(2)}) %collective-permute-start.1) | collective-permute-done | bytes 1572896 | tf_op jit(solution)/shard_map/ppermute | solution.py:408
  56.3 4.0 %collective-permute-start.2 = (bf16[1536,512]{1,0:T(8,128)(2,1)}, bf16[1536,512]{1,0:T(8,128)(2,1)S(1)}, u32[]{:S(2)}, u32[]{:S(2)}) collective-permute-start(bf16[1536,512]{1,0:T(8,128)(2,1)} %collective-permute-done.1.refs_0_.refs_4_), channel_id=1, source_target_pairs={{0,1},{1,0},{2,3},{3,2},{4,5},{5,4},{6,7},{7,6},{8,9},{9,8},{10,11... | collective-permute-start | bytes 4718600 | tf_op jit(solution)/shard_map/ppermute | solution.py:411
  60.4 5.1 %down.5.refs_2_ = bf16[672,3072]{1,0:T(8,128)(2,1)} custom-call(s32[3]{0:T(128)S(1)} %pad_add_fusion.where_ref, bf16[672,1536]{1,0:T(8,128)(2,1)S(1)} %get-tuple-element.42.here_ref, bf16[672,1536]{1,0:T(8,128)(2,1)S(1)} %collective-permute-done.there_ref, bf16[1536,512]{1,0:T(8,128)(2,1)} %bitcast.10.refs_0_, ...), custom_call_target="tpu_custom_call" | custom-call | flops 528482304 | bytes 1990656 | tf_op jit(solution)/shard_map/down/pallas_call | solution.py:346
  65.5 4.9 %down.6.refs_2_ = bf16[672,3072]{1,0:T(8,128)(2,1)} custom-call(s32[3]{0:T(128)S(1)} %pad_add_fusion.where_ref, bf16[672,1536]{1,0:T(8,128)(2,1)S(1)} %get-tuple-element.42.here_ref, bf16[672,1536]{1,0:T(8,128)(2,1)S(1)} %collective-permute-done.there_ref, bf16[1536,512]{1,0:T(8,128)(2,1)} %collective-permute-done.1.refs_0_.refs_4_, ...), custom_call_target="tpu_custom_call", output_to_operand_aliasing={{}: (5, {})} | custom-call | flops 528482304 | bytes 1990656 | tf_op jit(solution)/shard_map/down/pallas_call | solution.py:346
  70.4 5.6 %collective-permute-start.5 = (bf16[1536,768]{1,0:T(8,128)(2,1)}, bf16[1536,768]{1,0:T(8,128)(2,1)}, u32[]{:S(2)}, u32[]{:S(2)}) collective-permute-start(bf16[1536,768]{1,0:T(8,128)(2,1)} %bitcast.12.refs_2_.refs_0_), channel_id=1, source_target_pairs={{0,1},{1,0},{2,3},{3,2},{4,5},{5,4},{6,7},{7,6},{8,9},{9,8},{10,11... | collective-permute-start | bytes 7077896 | tf_op jit(solution)/shard_map/ppermute | solution.py:411
  76.0 0.8 collective-permute-start.4
  76.8 4.4 %all-to-all-start.2 = ((bf16[16,96,512]{2,1,0:T(8,128)(2,1)}), bf16[16,96,512]{2,1,0:T(8,128)(2,1)}, u32[]{:S(2)}, u32[]{:S(2)}) async-start(bf16[16,96,512]{2,1,0:T(8,128)(2,1)} %bitcast.35), calls=%async_computation.2 | async-start | bytes 3145728 | tf_op jit(solution)/shard_map/all_to_all | solution.py:404
  81.3 13.7 %raw.1.before_ref = f32[1344,1536]{1,0:T(8,128)} custom-call(s32[3]{0:T(128)} %copy-done.11, bf16[1536,512]{1,0:T(8,128)(2,1)} %bitcast.10.refs_0_, bf16[1344,3072]{1,0:T(8,128)(2,1)} %bitcast.41, bf16[1536,768]{1,0:T(8,128)(2,1)} %bitcast.12.refs_2_.refs_0_, bf16[1344,3072]{1,0:T(8,128)(2,1)} %bitcast.42, ...), custom_call_target="tpu_custom_call" | custom-call | flops 1849688064 | bytes 6709248 | tf_op jit(solution)/shard_map/raw/pallas_call | solution.py:235
  95.0 6.7 %down.7.refs_2_ = bf16[672,3072]{1,0:T(8,128)(2,1)} custom-call(s32[3]{0:T(128)S(1)} %copy-done.12, bf16[672,1536]{1,0:T(8,128)(2,1)S(1)} %get-tuple-element.42.here_ref, bf16[672,1536]{1,0:T(8,128)(2,1)S(1)} %copy-done.1, bf16[1536,768]{1,0:T(8,128)(2,1)} %bitcast.12.refs_2_.refs_0_, ...), custom_call_target="tpu_custom_call", output_to_operand_aliasing={{}: (5, {})} | custom-call | flops 792723456 | bytes 2469888 | tf_op jit(solution)/shard_map/down/pallas_call | solution.py:346
  102.0 3.3 %collective-permute-done.4.refs_0_ = bf16[1536,768]{1,0:T(8,128)(2,1)} collective-permute-done((bf16[1536,768]{1,0:T(8,128)(2,1)}, bf16[1536,768]{1,0:T(8,128)(2,1)}, u32[]{:S(2)}, u32[]{:S(2)}) %collective-permute-start.4) | collective-permute-done | bytes 2359328 | tf_op jit(solution)/shard_map/ppermute | solution.py:408
  106.1 16.4 %finish.1 = (bf16[1344,1536]{1,0:T(8,128)(2,1)}, bf16[1344,1536]{1,0:T(8,128)(2,1)}, f32[16,96]{1,0:T(8,128)}) custom-call(s32[3]{0:T(128)} %copy-done.11, bf16[1344,1536]{1,0:T(8,128)(2,1)} %bitcast.30, bf16[1344,1536]{1,0:T(8,128)(2,1)} %bitcast.32, f32[1344,1536]{1,0:T(8,128)} %raw.1.before_ref, bf16[1536,768]{1,0:T(8,128)(2,1)} %collective-permute-done.4.refs_0_, ...), custom_call_target="tpu_custom_call" | custom-call | flops 1321205760 | bytes 8036352 | tf_op jit(solution)/shard_map/finish/pallas_call | solution.py:290
  122.5 4.7 %all-to-all-start.3 = ((f32[16,1,96]{2,1,0:T(1,128)}), f32[16,1,96]{2,1,0:T(1,128)S(1)}, u32[]{:S(2)}, u32[]{:S(2)}) async-start(f32[16,1,96]{2,1,0:T(1,128)} %bitcast.51), calls=%async_computation.3 | async-start | bytes 16384 | tf_op jit(solution)/shard_map/all_to_all | solution.py:437
  127.3 1.6 %copy-done.2 = bf16[672,1536]{1,0:T(8,128)(2,1)S(1)} copy-done((bf16[672,1536]{1,0:T(8,128)(2,1)S(1)}, bf16[672,1536]{1,0:T(8,128)(2,1)}, u32[]{:S(2)}) %copy-start.2) | copy-done | bytes 2064408
  128.8 6.7 %down.8.refs_2_ = bf16[672,3072]{1,0:T(8,128)(2,1)} custom-call(s32[3]{0:T(128)S(1)} %copy-done.13, bf16[672,1536]{1,0:T(8,128)(2,1)S(1)} %get-tuple-element.42.here_ref, bf16[672,1536]{1,0:T(8,128)(2,1)S(1)} %copy-done.2, bf16[1536,768]{1,0:T(8,128)(2,1)} %collective-permute-done.4.refs_0_, ...), custom_call_target="tpu_custom_call", output_to_operand_aliasing={{}: (5, {})} | custom-call | flops 792723456 | bytes 2469888 | tf_op jit(solution)/shard_map/down/pallas_call | solution.py:346
  135.5 2.1 %collective-permute-start.9 = (f32[16,96]{1,0:T(8,128)S(1)}, f32[16,96]{1,0:T(8,128)S(1)}, u32[]{:S(2)}, u32[]{:S(2)}) collective-permute-start(f32[16,96]{1,0:T(8,128)S(1)} %bitcast.47), channel_id=1, source_target_pairs={{0,6},{2,0},{4,2},{6,4},{1,7},{3,1},{5,3},{7,5},{8,14},{10,8},{12,... | collective-permute-start | bytes 18440 | tf_op jit(solution)/shard_map/ppermute | solution.py:442
  138.3 1.6 %copy-done.3 = bf16[672,1536]{1,0:T(8,128)(2,1)S(1)} copy-done((bf16[672,1536]{1,0:T(8,128)(2,1)S(1)}, bf16[672,1536]{1,0:T(8,128)(2,1)}, u32[]{:S(2)}) %copy-start.3) | copy-done | bytes 2064408
  139.9 5.2 %down.9 = bf16[672,3072]{1,0:T(8,128)(2,1)} custom-call(s32[3]{0:T(128)S(1)} %copy-done.13, bf16[672,1536]{1,0:T(8,128)(2,1)S(1)} %get-tuple-element.42.here_ref, bf16[672,1536]{1,0:T(8,128)(2,1)S(1)} %copy-done.3, bf16[1536,512]{1,0:T(8,128)(2,1)} %bitcast.14.refs_2_.refs_0_, ...), custom_call_target="tpu_custom_call", output_to_operand_aliasing={{}: (5, {})} | custom-call | flops 528482304 | bytes 1990656 | tf_op jit(solution)/shard_map/down/pallas_call | solution.py:346
  145.7 1.8 %combine.1 = f32[4,256]{1,0:T(4,128)} custom-call(s32[4,256]{1,0:T(4,128)} %bitcast.37, bf16[4,256]{1,0:T(4,128)(2,1)} %bitcast.39, f32[16,256]{1,0:T(8,128)} %copy-done.15, f32[16,96]{1,0:T(8,128)} %bitcast.50, f32[16,96]{1,0:T(8,128)} %copy-done.21, f32[16,96]{1,0:T(8,128)} %copy-done.20, f32[16,96]{1,0:T(8,128)} %copy-done.19), custom_call_target="tpu_custom_call" | custom-call | tf_op jit(solution)/shard_map/combine/pallas_call | solution.py:380
  (55 shorter events, 4.1 us)
Async XLA Ops:
  0.7 64.8 %copy-start.11 = (s32[3]{0:T(128)}, s32[3]{0:T(128)S(1)}, u32[]{:S(2)}) copy-start(s32[3]{0:T(128)S(1)} %pad_add_fusion.where_ref) | copy-start | bytes 40
  0.7 1.4 copy-start.6
  3.5 11.1 %copy-start.7 = (bf16[256,3072]{1,0:T(8,128)(2,1)S(1)}, bf16[256,3072]{1,0:T(8,128)(2,1)}, u32[]{:S(2)}) copy-start(bf16[256,3072]{1,0:T(8,128)(2,1)} %grad_ref.5) | copy-start | bytes 4718596
  4.8 1.1 copy-start.10
  5.9 10.0 %copy-start.15 = (f32[16,256]{1,0:T(8,128)}, f32[16,256]{1,0:T(8,128)S(1)}, u32[]{:S(2)}) copy-start(f32[16,256]{1,0:T(8,128)S(1)} %get-tuple-element.58.slot_ref) | copy-start | bytes 49156
  5.9 29.3 %all-to-all-start = ((bf16[16,96,512]{2,1,0:T(8,128)(2,1)}), bf16[16,96,512]{2,1,0:T(8,128)(2,1)}, u32[]{:S(2)}, u32[]{:S(2)}) async-start(bf16[16,96,512]{2,1,0:T(8,128)(2,1)} %bitcast.36), calls=%async_computation | async-start | bytes 3145728 | tf_op jit(solution)/shard_map/all_to_all | solution.py:404
  14.6 5.5 %copy-start.5 = (bf16[1,1536,1344]{1,2,0:T(8,128)(2,1)S(1)}, bf16[1,1536,1344]{1,2,0:T(8,128)(2,1)}, u32[]{:S(2)}) copy-start(bf16[1,1536,1344]{1,2,0:T(8,128)(2,1)} %param.11) | copy-start | bytes 12386308
  15.9 1.2 copy-start.9
  17.1 3.0 %copy-start.4 = (bf16[1,1536,1344]{1,2,0:T(8,128)(2,1)S(1)}, bf16[1,1536,1344]{1,2,0:T(8,128)(2,1)}, u32[]{:S(2)}) copy-start(bf16[1,1536,1344]{1,2,0:T(8,128)(2,1)} %param.10) | copy-start | bytes 12386308
  18.7 1.4 copy-start.8
  23.9 1.3 copy-start.17
  35.3 21.1 %collective-permute-start.1 = (bf16[1536,512]{1,0:T(8,128)(2,1)}, bf16[1536,512]{1,0:T(8,128)(2,1)}, u32[]{:S(2)}, u32[]{:S(2)}) collective-permute-start(bf16[1536,512]{1,0:T(8,128)(2,1)} %bitcast.10.refs_0_), channel_id=1, source_target_pairs={{0,6},{2,0},{4,2},{6,4},{1,3},{3,5},{5,7},{7,1},{8,14},{10,8},{12,... | collective-permute-start | bytes 4718600 | tf_op jit(solution)/shard_map/ppermute | solution.py:408
  36.5 33.9 %all-to-all-start.1 = ((bf16[16,96,768]{2,1,0:T(8,128)(2,1)}), bf16[16,96,768]{2,1,0:T(8,128)(2,1)}, u32[]{:S(2)}, u32[]{:S(2)}) async-start(bf16[16,96,768]{2,1,0:T(8,128)(2,1)} %bitcast.34), calls=%async_computation.1 | async-start | bytes 4718592 | tf_op jit(solution)/shard_map/all_to_all | solution.py:404
  41.9 18.5 %collective-permute-start = (bf16[672,1536]{1,0:T(8,128)(2,1)}, bf16[672,1536]{1,0:T(8,128)(2,1)S(1)}, u32[]{:S(2)}, u32[]{:S(2)}) collective-permute-start(bf16[672,1536]{1,0:T(8,128)(2,1)} %copy-done.17), channel_id=1, source_target_pairs={{0,1},{1,0},{2,3},{3,2},{4,5},{5,4},{6,7},{7,6},{8,9},{9,8},{10,11... | collective-permute-start | bytes 6193160 | tf_op jit(solution)/shard_map/ppermute | solution.py:411
  46.7 13.7 %collective-permute-start.3 = (bf16[1536,512]{1,0:T(8,128)(2,1)}, bf16[1536,512]{1,0:T(8,128)(2,1)S(1)}, u32[]{:S(2)}, u32[]{:S(2)}) collective-permute-start(bf16[1536,512]{1,0:T(8,128)(2,1)} %bitcast.10.refs_0_), channel_id=1, source_target_pairs={{0,1},{1,0},{2,3},{3,2},{4,5},{5,4},{6,7},{7,6},{8,9},{9,8},{10,11... | collective-permute-start | bytes 4718600 | tf_op jit(solution)/shard_map/ppermute | solution.py:411
  56.3 9.1 %collective-permute-start.2 = (bf16[1536,512]{1,0:T(8,128)(2,1)}, bf16[1536,512]{1,0:T(8,128)(2,1)S(1)}, u32[]{:S(2)}, u32[]{:S(2)}) collective-permute-start(bf16[1536,512]{1,0:T(8,128)(2,1)} %collective-permute-done.1.refs_0_.refs_4_), channel_id=1, source_target_pairs={{0,1},{1,0},{2,3},{3,2},{4,5},{5,4},{6,7},{7,6},{8,9},{9,8},{10,11... | collective-permute-start | bytes 4718600 | tf_op jit(solution)/shard_map/ppermute | solution.py:411
  60.4 5.1 %copy-start = (bf16[672,1536]{1,0:T(8,128)(2,1)}, bf16[672,1536]{1,0:T(8,128)(2,1)S(1)}, u32[]{:S(2)}) copy-start(bf16[672,1536]{1,0:T(8,128)(2,1)S(1)} %collective-permute-done.there_ref) | copy-start | bytes 6193156
  70.4 24.6 %collective-permute-start.5 = (bf16[1536,768]{1,0:T(8,128)(2,1)}, bf16[1536,768]{1,0:T(8,128)(2,1)}, u32[]{:S(2)}, u32[]{:S(2)}) collective-permute-start(bf16[1536,768]{1,0:T(8,128)(2,1)} %bitcast.12.refs_2_.refs_0_), channel_id=1, source_target_pairs={{0,1},{1,0},{2,3},{3,2},{4,5},{5,4},{6,7},{7,6},{8,9},{9,8},{10,11... | collective-permute-start | bytes 7077896 | tf_op jit(solution)/shard_map/ppermute | solution.py:411
  76.0 29.2 %collective-permute-start.4 = (bf16[1536,768]{1,0:T(8,128)(2,1)}, bf16[1536,768]{1,0:T(8,128)(2,1)}, u32[]{:S(2)}, u32[]{:S(2)}) collective-permute-start(bf16[1536,768]{1,0:T(8,128)(2,1)} %bitcast.12.refs_2_.refs_0_), channel_id=1, source_target_pairs={{0,6},{2,0},{4,2},{6,4},{1,3},{3,5},{5,7},{7,1},{8,14},{10,8},{12,... | collective-permute-start | bytes 7077896 | tf_op jit(solution)/shard_map/ppermute | solution.py:408
  76.8 25.1 %all-to-all-start.2 = ((bf16[16,96,512]{2,1,0:T(8,128)(2,1)}), bf16[16,96,512]{2,1,0:T(8,128)(2,1)}, u32[]{:S(2)}, u32[]{:S(2)}) async-start(bf16[16,96,512]{2,1,0:T(8,128)(2,1)} %bitcast.35), calls=%async_computation.2 | async-start | bytes 3145728 | tf_op jit(solution)/shard_map/all_to_all | solution.py:404
  81.2 13.8 %copy-start.1 = (bf16[672,1536]{1,0:T(8,128)(2,1)S(1)}, bf16[672,1536]{1,0:T(8,128)(2,1)}, u32[]{:S(2)}) copy-start(bf16[672,1536]{1,0:T(8,128)(2,1)} %copy-done) | copy-start | bytes 6193156
  81.3 13.8 %copy-start.12 = (s32[3]{0:T(128)S(1)}, s32[3]{0:T(128)}, u32[]{:S(2)}) copy-start(s32[3]{0:T(128)} %copy-done.11) | copy-start | bytes 40
  105.2 22.0 %copy-start.13 = (s32[3]{0:T(128)S(1)}, s32[3]{0:T(128)}, u32[]{:S(2)}) copy-start(s32[3]{0:T(128)} %copy-done.11) | copy-start | bytes 40
  105.2 22.0 %collective-permute-start.6 = (bf16[1536,768]{1,0:T(8,128)(2,1)}, bf16[1536,768]{1,0:T(8,128)(2,1)}, u32[]{:S(2)}, u32[]{:S(2)}) collective-permute-start(bf16[1536,768]{1,0:T(8,128)(2,1)} %collective-permute-done.4.refs_0_), channel_id=1, source_target_pairs={{0,1},{1,0},{2,3},{3,2},{4,5},{5,4},{6,7},{7,6},{8,9},{9,8},{10,11... | collective-permute-start | bytes 7077896 | tf_op jit(solution)/shard_map/ppermute | solution.py:411
  106.0 32.3 %collective-permute-start.10 = (bf16[1536,512]{1,0:T(8,128)(2,1)}, bf16[1536,512]{1,0:T(8,128)(2,1)}, u32[]{:S(2)}, u32[]{:S(2)}) collective-permute-start(bf16[1536,512]{1,0:T(8,128)(2,1)} %bitcast.14.refs_2_.refs_0_), channel_id=1, source_target_pairs={{0,1},{1,0},{2,3},{3,2},{4,5},{5,4},{6,7},{7,6},{8,9},{9,8},{10,11... | collective-permute-start | bytes 4718600 | tf_op jit(solution)/shard_map/ppermute | solution.py:411
  122.5 13.0 %all-to-all-start.3 = ((f32[16,1,96]{2,1,0:T(1,128)}), f32[16,1,96]{2,1,0:T(1,128)S(1)}, u32[]{:S(2)}, u32[]{:S(2)}) async-start(f32[16,1,96]{2,1,0:T(1,128)} %bitcast.51), calls=%async_computation.3 | async-start | bytes 16384 | tf_op jit(solution)/shard_map/all_to_all | solution.py:437
  127.3 1.6 %copy-start.2 = (bf16[672,1536]{1,0:T(8,128)(2,1)S(1)}, bf16[672,1536]{1,0:T(8,128)(2,1)}, u32[]{:S(2)}) copy-start(bf16[672,1536]{1,0:T(8,128)(2,1)} %copy-done) | copy-start | bytes 6193156
  135.5 9.5 %copy-start.18 = (f32[16,1,96]{2,1,0:T(1,128)}, f32[16,1,96]{2,1,0:T(1,128)S(1)}, u32[]{:S(2)}) copy-start(f32[16,1,96]{2,1,0:T(1,128)S(1)} %all-to-all-done.3) | copy-start | bytes 18436
  135.5 9.5 %collective-permute-start.9 = (f32[16,96]{1,0:T(8,128)S(1)}, f32[16,96]{1,0:T(8,128)S(1)}, u32[]{:S(2)}, u32[]{:S(2)}) collective-permute-start(f32[16,96]{1,0:T(8,128)S(1)} %bitcast.47), channel_id=1, source_target_pairs={{0,6},{2,0},{4,2},{6,4},{1,7},{3,1},{5,3},{7,5},{8,14},{10,8},{12,... | collective-permute-start | bytes 18440 | tf_op jit(solution)/shard_map/ppermute | solution.py:442
  137.6 7.5 %collective-permute-start.8 = (f32[16,96]{1,0:T(8,128)S(1)}, f32[16,96]{1,0:T(8,128)S(1)}, u32[]{:S(2)}, u32[]{:S(2)}) collective-permute-start(f32[16,96]{1,0:T(8,128)S(1)} %bitcast.48), channel_id=1, source_target_pairs={{0,4},{2,6},{4,0},{6,2},{1,5},{3,7},{5,1},{7,3},{8,12},{10,14},{12... | collective-permute-start | bytes 18440 | tf_op jit(solution)/shard_map/ppermute | solution.py:442
  137.6 7.5 %collective-permute-start.7 = (f32[16,96]{1,0:T(8,128)S(1)}, f32[16,96]{1,0:T(8,128)S(1)}, u32[]{:S(2)}, u32[]{:S(2)}) collective-permute-start(f32[16,96]{1,0:T(8,128)S(1)} %bitcast.49), channel_id=1, source_target_pairs={{0,2},{2,4},{4,6},{6,0},{1,3},{3,5},{5,7},{7,1},{8,10},{10,12},{12... | collective-permute-start | bytes 18440 | tf_op jit(solution)/shard_map/ppermute | solution.py:442
  138.3 1.6 %copy-start.3 = (bf16[672,1536]{1,0:T(8,128)(2,1)S(1)}, bf16[672,1536]{1,0:T(8,128)(2,1)}, u32[]{:S(2)}) copy-start(bf16[672,1536]{1,0:T(8,128)(2,1)} %copy-done) | copy-start | bytes 6193156
  (5 other events, 3.2 us)

commit v4 on v3

--- a/solution.py
+++ b/solution.py
@@ -277,12 +277,14 @@
     @pl.when(pl.program_id(0) == pl.num_programs(0) - 1)
     def _():
         total = jnp.sum(acc[...], axis=0, keepdims=True)
-        groups, capacity = part_ref.shape
+        copies, groups, capacity = part_ref.shape
         for g in range(groups):
-            part_ref[g : g + 1, :] = total[:, g * capacity : (g + 1) * capacity]
-
-
-def finish(where, gate, up, before, w, pieces, groups):
+            sums = total[:, g * capacity : (g + 1) * capacity]
+            for x in range(copies):
+                part_ref[x, g : g + 1, :] = sums
+
+
+def finish(where, gate, up, before, w, pieces, groups, copies):
     ff, slots = gate.shape
     depth = sum(chunk[1] for _, chunk, _ in pieces)
     tile = pl.BlockSpec((TILE_FF, slots), lambda n, s: (n, 0))
@@ -292,11 +294,11 @@
         "finish",
         (ff // TILE_FF,),
         [tile, tile, tile] + piece_specs(pieces, slots),
-        [tile, tile, pl.BlockSpec((groups, slots // groups), fixed)],
+        [tile, tile, pl.BlockSpec((copies, groups, slots // groups), lambda n, s: (0, 0, 0))],
         [
             jax.ShapeDtypeStruct((ff, slots), BF16),
             jax.ShapeDtypeStruct((ff, slots), BF16),
-            jax.ShapeDtypeStruct((groups, slots // groups), F32),
+            jax.ShapeDtypeStruct((copies, groups, slots // groups), F32),
         ],
         [pltpu.VMEM((8, slots), F32)],
         2 * slots * ff * depth,
@@ -357,11 +359,10 @@
     )(*args)
 
 
-def combine_kernel(experts, route_ref, prob_ref, slot_ref, *refs):
-    out_ref = refs[-1]
-    values = refs[0][...]
-    for ref in refs[1:-1]:
-        values += ref[...]
+def combine_kernel(experts, route_ref, prob_ref, slot_ref, values_ref, out_ref):
+    values = values_ref[0]
+    for x in range(1, values_ref.shape[0]):
+        values += values_ref[x]
     capacity = values.shape[1]
     tokens = route_ref.shape[1]
     columns = values.T
@@ -376,12 +377,12 @@
 
 
 def combine(route, prob, slot, values):
-    experts = values[0].shape[0]
+    experts = values.shape[1]
     return pl.pallas_call(
         functools.partial(combine_kernel, experts),
         out_shape=jax.ShapeDtypeStruct(route.shape, F32),
         name="combine",
-    )(route, prob, slot, *values)
+    )(route, prob, slot, values)
 
 
 def local(out_grad, route, gate_prob, w_down, gate_pre, up_pre):
@@ -390,9 +391,8 @@
     slots, ff = gate_pre.shape[1:]
     capacity = slots // experts
     width = out_grad.shape[1]
-    where = jnp.stack(
-        [lax.axis_index("etp") % 2, lax.axis_index("expert"), lax.axis_index("dp")]
-    ).astype(jnp.int32)
+    parity = lax.bitwise_and(lax.axis_index("etp"), 1).reshape(1)
+    where = jnp.concatenate([parity, parity, lax.axis_index("dp").reshape(1)])
     gate, up, w = gate_pre[0].T, up_pre[0].T, w_down[0]
     route, prob = route.T, gate_prob.T
 
@@ -411,11 +411,11 @@
         return lax.ppermute(x, "dp", [(0, 1), (1, 0)])
 
     c0, c1 = SHARED
-    first, slot, pick = dispatch(where, route, prob, out_grad, experts, capacity)
+    first, slot, pick = dispatch(parity, route, prob, out_grad, experts, capacity)
     gate, up, pick = lax.optimization_barrier((gate, up, pick))
     own0 = fetch(first)
-    send1 = dispatch_more(where, pick, out_grad, c1, OWN)
-    send2 = dispatch_more(where, pick, out_grad, DIRECT, SAME)
+    send1 = dispatch_more(parity, pick, out_grad, c1, OWN)
+    send2 = dispatch_more(parity, pick, out_grad, DIRECT, SAME)
     act_other, act_mine = activation(where, gate, up)
     own0, send1, send2, act_other, act_mine = lax.optimization_barrier(
         (own0, send1, send2, act_other, act_mine)
@@ -433,17 +433,13 @@
     total = down(where, acts, pieces, width, total)
     direct, oth1, raw, total = lax.optimization_barrier((direct, oth1, raw, total))
     late = [(oth1, c1, OTHER), (direct, DIRECT, SAME)]
-    grad_gate, grad_up, sums = finish(where, gate, up, raw, w, late, experts)
-    back = lax.all_to_all(sums, "expert", split_axis=0, concat_axis=0, tiled=True)
+    grad_gate, grad_up, sums = finish(where, gate, up, raw, w, late, experts, etp)
+    sums = sums.reshape(etp * experts, capacity)
+    back = lax.all_to_all(sums, ("etp", "expert"), split_axis=0, concat_axis=0, tiled=True)
     pieces = [(rows, swap_dp(rows), chunk, side) for rows, chunk, side in late]
-    total = down(where, acts, pieces[:1], width, total)
+    total = down(where, acts, pieces, width, total)
     back, total = lax.optimization_barrier((back, total))
-    others = [
-        lax.ppermute(back, "etp", [(i, (i + k) % etp) for i in range(etp)]) for k in range(1, etp)
-    ]
-    total = down(where, acts, pieces[1:], width, total)
-    others, total = lax.optimization_barrier((others, total))
-    grad_prob = combine(route, prob, slot, [back, *others])
+    grad_prob = combine(route, prob, slot, back.reshape(etp, experts, capacity))
     return grad_gate.T[None], grad_up.T[None], total[None], grad_prob.T
 
 

time: 149 us -> 144 us (0.966)
  Pallas kernels: 68.5 us -> 65.1 us
  waiting for transfers between devices: 23.2 us -> 19.9 us
  local copies, waits for them, and re-layouts: 11.6 us -> 14.3 us
    all_to_all x3, waiting for transfers between devices: 10.3 us -> 7.01 us  [fetch(): x = lax.all_to_all(x, 'expert', split_axis=0, concat_axis=0, tiled=True)]
    ppermute x3 -> x0, starting transfers between devices: 2.79 us -> none  [local(): lax.ppermute(back, 'etp', [(i, (i + k) % etp) for i in range(etp)])]
    unnamed x44 -> x36, local copies, waits for them, and re-layouts: 11.6 us -> 14.3 us
    all_to_all x1, starting transfers between devices: 4.7 us -> 7.39 us  [local(): lax.all_to_all(sums, ('etp', 'expert'), split_axis=0, concat_axis=0, tile...]
    pallas_call x5 -> x4, Pallas kernels: 28.5 us -> 26.7 us  [down(): call(functools.partial(down_kernel, counts), 'down', (tiles,), in_specs,...]
  transfers between devices with their start and end apart: 15 -> 12, of which waited for: 4 -> 4; matrix products, arithmetic and copies ran while one was open for 0% -> 0% of each run, Pallas kernels for 44% -> 44%
where the time goes in v4:
time: 144 us; the launch traced here: 143 us
  Pallas kernels  65.1 us (45%)
  starting transfers between devices  43.2 us (30%)
  waiting for transfers between devices  19.9 us (14%)
  local copies, waits for them, and re-layouts  14.3 us (10%)
    pallas_call x4, Pallas kernels, down(): call(functools.partial(down_kernel, counts), 'down', (tiles,), in_specs,...  26.7 us
    all_to_all x3, starting transfers between devices, fetch(): x = lax.all_to_all(x, 'expert', split_axis=0, concat_axis=0, tiled=True)  18.4 us
    pallas_call x1, Pallas kernels, finish(): call(functools.partial(finish_kernel, len(pieces)), 'finish', (ff // TILE...  16.4 us
    ppermute x6, starting transfers between devices, swap_dp(): return lax.ppermute(x, 'dp', [(0, 1), (1, 0)])  15.4 us
    unnamed x36, local copies, waits for them, and re-layouts  14.3 us
    pallas_call x1, Pallas kernels, raw_part(): call(functools.partial(raw_kernel, len(pieces), more), 'raw', (ff // TILE...  13.8 us
    ppermute x2, waiting for transfers between devices, beside(): return lax.ppermute(x, ('etp', 'dp'), swap)  12.8 us
    all_to_all x1, starting transfers between devices, local(): lax.all_to_all(sums, ('etp', 'expert'), split_axis=0, concat_axis=0, tile...  7.39 us
  transfers between devices with their start and end apart: 12, of which 4 were waited for; matrix products, arithmetic and copies ran while one was open for 0% of the time, Pallas kernels for 44%

profile of v4, /device:TPU:1, one launch (start us, length us, event | category | flops | bytes accessed | tf_op | source)
XLA Modules:
  0.0 143.4 jit_solution(10564308715816648296)
XLA Ops:
  0.6 1.4 copy-done.5
  3.4 0.7 dispatch.1
  4.2 1.1 copy-done.9
  5.3 8.6 %all-to-all-start = ((bf16[16,96,512]{2,1,0:T(8,128)(2,1)}), bf16[16,96,512]{2,1,0:T(8,128)(2,1)}, u32[]{:S(2)}, u32[]{:S(2)}) async-start(bf16[16,96,512]{2,1,0:T(8,128)(2,1)} %bitcast.36), calls=%async_computation | async-start | bytes 3145728 | tf_op jit(solution)/shard_map/all_to_all | solution.py:404
  14.0 1.0 dispatch_more.2
  15.0 1.4 copy-done.7
  16.4 0.8 dispatch_more.3
  17.2 1.2 copy-done.8
  18.4 2.2 %copy-done.3 = bf16[1,1536,1344]{1,2,0:T(8,128)(2,1)S(1)} copy-done((bf16[1,1536,1344]{1,2,0:T(8,128)(2,1)S(1)}, bf16[1,1536,1344]{1,2,0:T(8,128)(2,1)}, u32[]{:S(2)}) %copy-start.3) | copy-done | bytes 4128792
  20.6 2.2 %copy-done.4 = bf16[1,1536,1344]{1,2,0:T(8,128)(2,1)S(1)} copy-done((bf16[1,1536,1344]{1,2,0:T(8,128)(2,1)S(1)}, bf16[1,1536,1344]{1,2,0:T(8,128)(2,1)}, u32[]{:S(2)}) %copy-start.4) | copy-done | bytes 4128792
  22.8 3.8 %activation.1 = (bf16[672,1536]{1,0:T(8,128)(2,1)S(1)}, bf16[672,1536]{1,0:T(8,128)(2,1)S(1)}) custom-call(s32[3]{0:T(128)S(1)} %pad_add_fusion.where_ref, bf16[1344,1536]{1,0:T(8,128)(2,1)S(1)} %bitcast.31, bf16[1344,1536]{1,0:T(8,128)(2,1)S(1)} %bitcast.33), custom_call_target="tpu_custom_call" | custom-call | flops 1 | bytes 1 | tf_op jit(solution)/shard_map/activation/pallas_call | solution.py:182
  26.6 1.3 copy-done.16
  27.9 6.8 %all-to-all-done = bf16[16,96,512]{2,1,0:T(8,128)(2,1)} async-done(((bf16[16,96,512]{2,1,0:T(8,128)(2,1)}), bf16[16,96,512]{2,1,0:T(8,128)(2,1)}, u32[]{:S(2)}, u32[]{:S(2)}) %all-to-all-start) | async-done | bytes 1572896 | tf_op jit(solution)/shard_map/all_to_all | solution.py:404
  34.6 1.2 collective-permute-start.1
  35.9 5.4 %all-to-all-start.1 = ((bf16[16,96,768]{2,1,0:T(8,128)(2,1)}), bf16[16,96,768]{2,1,0:T(8,128)(2,1)}, u32[]{:S(2)}, u32[]{:S(2)}) async-start(bf16[16,96,768]{2,1,0:T(8,128)(2,1)} %bitcast.34), calls=%async_computation.1 | async-start | bytes 4718592 | tf_op jit(solution)/shard_map/all_to_all | solution.py:404
  41.2 4.8 %collective-permute-start = (bf16[672,1536]{1,0:T(8,128)(2,1)}, bf16[672,1536]{1,0:T(8,128)(2,1)S(1)}, u32[]{:S(2)}, u32[]{:S(2)}) collective-permute-start(bf16[672,1536]{1,0:T(8,128)(2,1)} %copy-done.16), channel_id=1, source_target_pairs={{0,1},{1,0},{2,3},{3,2},{4,5},{5,4},{6,7},{7,6},{8,9},{9,8},{10,11... | collective-permute-start | bytes 6193160 | tf_op jit(solution)/shard_map/ppermute | solution.py:411
  46.1 9.6 %collective-permute-done.1.refs_0_.refs_4_ = bf16[1536,512]{1,0:T(8,128)(2,1)} collective-permute-done((bf16[1536,512]{1,0:T(8,128)(2,1)}, bf16[1536,512]{1,0:T(8,128)(2,1)}, u32[]{:S(2)}, u32[]{:S(2)}) %collective-permute-start.1) | collective-permute-done | bytes 1572896 | tf_op jit(solution)/shard_map/ppermute | solution.py:408
  55.7 4.0 %collective-permute-start.2 = (bf16[1536,512]{1,0:T(8,128)(2,1)}, bf16[1536,512]{1,0:T(8,128)(2,1)S(1)}, u32[]{:S(2)}, u32[]{:S(2)}) collective-permute-start(bf16[1536,512]{1,0:T(8,128)(2,1)} %collective-permute-done.1.refs_0_.refs_4_), channel_id=1, source_target_pairs={{0,1},{1,0},{2,3},{3,2},{4,5},{5,4},{6,7},{7,6},{8,9},{9,8},{10,11... | collective-permute-start | bytes 4718600 | tf_op jit(solution)/shard_map/ppermute | solution.py:411
  59.8 5.1 %down.4.refs_2_ = bf16[672,3072]{1,0:T(8,128)(2,1)} custom-call(s32[3]{0:T(128)S(1)} %pad_add_fusion.where_ref, bf16[672,1536]{1,0:T(8,128)(2,1)S(1)} %get-tuple-element.38.here_ref, bf16[672,1536]{1,0:T(8,128)(2,1)S(1)} %collective-permute-done.there_ref, bf16[1536,512]{1,0:T(8,128)(2,1)} %bitcast.9.refs_0_, ...), custom_call_target="tpu_custom_call" | custom-call | flops 528482304 | bytes 1990656 | tf_op jit(solution)/shard_map/down/pallas_call | solution.py:348
  64.8 4.9 %down.5.refs_2_ = bf16[672,3072]{1,0:T(8,128)(2,1)} custom-call(s32[3]{0:T(128)S(1)} %pad_add_fusion.where_ref, bf16[672,1536]{1,0:T(8,128)(2,1)S(1)} %get-tuple-element.38.here_ref, bf16[672,1536]{1,0:T(8,128)(2,1)S(1)} %collective-permute-done.there_ref, bf16[1536,512]{1,0:T(8,128)(2,1)} %collective-permute-done.1.refs_0_.refs_4_, ...), custom_call_target="tpu_custom_call", output_to_operand_aliasing={{}: (5, {})} | custom-call | flops 528482304 | bytes 1990656 | tf_op jit(solution)/shard_map/down/pallas_call | solution.py:348
  69.8 5.6 %collective-permute-start.5 = (bf16[1536,768]{1,0:T(8,128)(2,1)}, bf16[1536,768]{1,0:T(8,128)(2,1)}, u32[]{:S(2)}, u32[]{:S(2)}) collective-permute-start(bf16[1536,768]{1,0:T(8,128)(2,1)} %bitcast.11.refs_2_.refs_0_), channel_id=1, source_target_pairs={{0,1},{1,0},{2,3},{3,2},{4,5},{5,4},{6,7},{7,6},{8,9},{9,8},{10,11... | collective-permute-start | bytes 7077896 | tf_op jit(solution)/shard_map/ppermute | solution.py:411
  75.4 0.8 collective-permute-start.4
  76.2 4.4 %all-to-all-start.2 = ((bf16[16,96,512]{2,1,0:T(8,128)(2,1)}), bf16[16,96,512]{2,1,0:T(8,128)(2,1)}, u32[]{:S(2)}, u32[]{:S(2)}) async-start(bf16[16,96,512]{2,1,0:T(8,128)(2,1)} %bitcast.35), calls=%async_computation.2 | async-start | bytes 3145728 | tf_op jit(solution)/shard_map/all_to_all | solution.py:404
  80.6 13.8 %raw.1.before_ref = f32[1344,1536]{1,0:T(8,128)} custom-call(s32[3]{0:T(128)} %copy-done.10, bf16[1536,512]{1,0:T(8,128)(2,1)} %bitcast.9.refs_0_, bf16[1344,3072]{1,0:T(8,128)(2,1)} %bitcast.41, bf16[1536,768]{1,0:T(8,128)(2,1)} %bitcast.11.refs_2_.refs_0_, bf16[1344,3072]{1,0:T(8,128)(2,1)} %bitcast.42, ...), custom_call_target="tpu_custom_call" | custom-call | flops 1849688064 | bytes 6709248 | tf_op jit(solution)/shard_map/raw/pallas_call | solution.py:235
  94.4 6.7 %down.6.refs_4_ = bf16[672,3072]{1,0:T(8,128)(2,1)} custom-call(s32[3]{0:T(128)S(1)} %copy-done.11, bf16[672,1536]{1,0:T(8,128)(2,1)S(1)} %get-tuple-element.38.here_ref, bf16[672,1536]{1,0:T(8,128)(2,1)S(1)} %copy-done.1, bf16[1536,768]{1,0:T(8,128)(2,1)} %bitcast.11.refs_2_.refs_0_, ...), custom_call_target="tpu_custom_call", output_to_operand_aliasing={{}: (5, {})} | custom-call | flops 792723456 | bytes 2469888 | tf_op jit(solution)/shard_map/down/pallas_call | solution.py:348
  101.3 3.2 %collective-permute-done.4.refs_0_ = bf16[1536,768]{1,0:T(8,128)(2,1)} collective-permute-done((bf16[1536,768]{1,0:T(8,128)(2,1)}, bf16[1536,768]{1,0:T(8,128)(2,1)}, u32[]{:S(2)}, u32[]{:S(2)}) %collective-permute-start.4) | collective-permute-done | bytes 2359328 | tf_op jit(solution)/shard_map/ppermute | solution.py:408
  104.6 0.8 collective-permute-start.6
  105.4 16.4 %finish.1 = (bf16[1344,1536]{1,0:T(8,128)(2,1)}, bf16[1344,1536]{1,0:T(8,128)(2,1)}, f32[4,16,96]{2,1,0:T(8,128)}) custom-call(s32[3]{0:T(128)} %copy-done.10, bf16[1344,1536]{1,0:T(8,128)(2,1)} %bitcast.30, bf16[1344,1536]{1,0:T(8,128)(2,1)} %bitcast.32, f32[1344,1536]{1,0:T(8,128)} %raw.1.before_ref, bf16[1536,768]{1,0:T(8,128)(2,1)} %collective-permute-done.4.refs_0_, ...), custom_call_target="tpu_custom_call" | custom-call | flops 1321205760 | bytes 8036352 | tf_op jit(solution)/shard_map/finish/pallas_call | solution.py:292
  121.9 7.4 %all-to-all-start.3 = ((f32[64,1,96]{2,1,0:T(1,128)}), f32[64,1,96]{2,1,0:T(1,128)S(1)}, u32[]{:S(2)}, u32[]{:S(2)}) async-start(f32[64,1,96]{2,1,0:T(1,128)} %bitcast.48), calls=%async_computation.3 | async-start | bytes 65536 | tf_op jit(solution)/shard_map/all_to_all | solution.py:438
  129.3 1.6 %copy-done.2 = bf16[672,1536]{1,0:T(8,128)(2,1)S(1)} copy-done((bf16[672,1536]{1,0:T(8,128)(2,1)S(1)}, bf16[672,1536]{1,0:T(8,128)(2,1)}, u32[]{:S(2)}) %copy-start.2) | copy-done | bytes 2064408
  130.9 10.0 %down.7 = bf16[672,3072]{1,0:T(8,128)(2,1)} custom-call(s32[3]{0:T(128)S(1)} %copy-done.12, bf16[672,1536]{1,0:T(8,128)(2,1)S(1)} %get-tuple-element.38.here_ref, bf16[672,1536]{1,0:T(8,128)(2,1)S(1)} %copy-done.2, bf16[1536,768]{1,0:T(8,128)(2,1)} %collective-permute-done.4.refs_0_, ...), custom_call_target="tpu_custom_call", output_to_operand_aliasing={{}: (7, {})} | custom-call | flops 1321205760 | bytes 3428352 | tf_op jit(solution)/shard_map/down/pallas_call | solution.py:348
  141.6 1.8 %combine.1 = f32[4,256]{1,0:T(4,128)} custom-call(s32[4,256]{1,0:T(4,128)} %bitcast.37, bf16[4,256]{1,0:T(4,128)(2,1)} %bitcast.39, f32[16,256]{1,0:T(8,128)} %copy-done.14, f32[4,16,96]{2,1,0:T(8,128)} %bitcast.47), custom_call_target="tpu_custom_call" | custom-call | tf_op jit(solution)/shard_map/combine/pallas_call | solution.py:381
  (40 shorter events, 2.6 us)
Async XLA Ops:
  0.6 1.4 copy-start.5
  2.0 0.7 copy-start.13
  2.7 0.7 copy-start.15
  3.4 10.5 %copy-start.6 = (bf16[256,3072]{1,0:T(8,128)(2,1)S(1)}, bf16[256,3072]{1,0:T(8,128)(2,1)}, u32[]{:S(2)}) copy-start(bf16[256,3072]{1,0:T(8,128)(2,1)} %grad_ref.5) | copy-start | bytes 4718596
  4.2 1.1 copy-start.9
  5.3 8.7 %copy-start.14 = (f32[16,256]{1,0:T(8,128)}, f32[16,256]{1,0:T(8,128)S(1)}, u32[]{:S(2)}) copy-start(f32[16,256]{1,0:T(8,128)S(1)} %get-tuple-element.52.slot_ref) | copy-start | bytes 49156
  5.3 29.3 %all-to-all-start = ((bf16[16,96,512]{2,1,0:T(8,128)(2,1)}), bf16[16,96,512]{2,1,0:T(8,128)(2,1)}, u32[]{:S(2)}, u32[]{:S(2)}) async-start(bf16[16,96,512]{2,1,0:T(8,128)(2,1)} %bitcast.36), calls=%async_computation | async-start | bytes 3145728 | tf_op jit(solution)/shard_map/all_to_all | solution.py:404
  15.0 1.4 copy-start.7
  17.2 1.2 copy-start.8
  18.4 2.2 %copy-start.3 = (bf16[1,1536,1344]{1,2,0:T(8,128)(2,1)S(1)}, bf16[1,1536,1344]{1,2,0:T(8,128)(2,1)}, u32[]{:S(2)}) copy-start(bf16[1,1536,1344]{1,2,0:T(8,128)(2,1)} %param.10) | copy-start | bytes 12386308
  20.6 2.2 %copy-start.4 = (bf16[1,1536,1344]{1,2,0:T(8,128)(2,1)S(1)}, bf16[1,1536,1344]{1,2,0:T(8,128)(2,1)}, u32[]{:S(2)}) copy-start(bf16[1,1536,1344]{1,2,0:T(8,128)(2,1)} %param.11) | copy-start | bytes 12386308
  22.8 42.1 %copy-start.10 = (s32[3]{0:T(128)}, s32[3]{0:T(128)S(1)}, u32[]{:S(2)}) copy-start(s32[3]{0:T(128)S(1)} %pad_add_fusion.where_ref) | copy-start | bytes 40
  26.6 1.3 copy-start.16
  34.6 21.1 %collective-permute-start.1 = (bf16[1536,512]{1,0:T(8,128)(2,1)}, bf16[1536,512]{1,0:T(8,128)(2,1)}, u32[]{:S(2)}, u32[]{:S(2)}) collective-permute-start(bf16[1536,512]{1,0:T(8,128)(2,1)} %bitcast.9.refs_0_), channel_id=1, source_target_pairs={{0,6},{2,0},{4,2},{6,4},{1,3},{3,5},{5,7},{7,1},{8,14},{10,8},{12,... | collective-permute-start | bytes 4718600 | tf_op jit(solution)/shard_map/ppermute | solution.py:408
  35.9 33.9 %all-to-all-start.1 = ((bf16[16,96,768]{2,1,0:T(8,128)(2,1)}), bf16[16,96,768]{2,1,0:T(8,128)(2,1)}, u32[]{:S(2)}, u32[]{:S(2)}) async-start(bf16[16,96,768]{2,1,0:T(8,128)(2,1)} %bitcast.34), calls=%async_computation.1 | async-start | bytes 4718592 | tf_op jit(solution)/shard_map/all_to_all | solution.py:404
  41.2 18.5 %collective-permute-start = (bf16[672,1536]{1,0:T(8,128)(2,1)}, bf16[672,1536]{1,0:T(8,128)(2,1)S(1)}, u32[]{:S(2)}, u32[]{:S(2)}) collective-permute-start(bf16[672,1536]{1,0:T(8,128)(2,1)} %copy-done.16), channel_id=1, source_target_pairs={{0,1},{1,0},{2,3},{3,2},{4,5},{5,4},{6,7},{7,6},{8,9},{9,8},{10,11... | collective-permute-start | bytes 6193160 | tf_op jit(solution)/shard_map/ppermute | solution.py:411
  46.0 13.7 %collective-permute-start.3 = (bf16[1536,512]{1,0:T(8,128)(2,1)}, bf16[1536,512]{1,0:T(8,128)(2,1)S(1)}, u32[]{:S(2)}, u32[]{:S(2)}) collective-permute-start(bf16[1536,512]{1,0:T(8,128)(2,1)} %bitcast.9.refs_0_), channel_id=1, source_target_pairs={{0,1},{1,0},{2,3},{3,2},{4,5},{5,4},{6,7},{7,6},{8,9},{9,8},{10,11... | collective-permute-start | bytes 4718600 | tf_op jit(solution)/shard_map/ppermute | solution.py:411
  55.7 9.1 %collective-permute-start.2 = (bf16[1536,512]{1,0:T(8,128)(2,1)}, bf16[1536,512]{1,0:T(8,128)(2,1)S(1)}, u32[]{:S(2)}, u32[]{:S(2)}) collective-permute-start(bf16[1536,512]{1,0:T(8,128)(2,1)} %collective-permute-done.1.refs_0_.refs_4_), channel_id=1, source_target_pairs={{0,1},{1,0},{2,3},{3,2},{4,5},{5,4},{6,7},{7,6},{8,9},{9,8},{10,11... | collective-permute-start | bytes 4718600 | tf_op jit(solution)/shard_map/ppermute | solution.py:411
  59.8 5.1 %copy-start = (bf16[672,1536]{1,0:T(8,128)(2,1)}, bf16[672,1536]{1,0:T(8,128)(2,1)S(1)}, u32[]{:S(2)}) copy-start(bf16[672,1536]{1,0:T(8,128)(2,1)S(1)} %collective-permute-done.there_ref) | copy-start | bytes 6193156
  69.8 24.6 %collective-permute-start.5 = (bf16[1536,768]{1,0:T(8,128)(2,1)}, bf16[1536,768]{1,0:T(8,128)(2,1)}, u32[]{:S(2)}, u32[]{:S(2)}) collective-permute-start(bf16[1536,768]{1,0:T(8,128)(2,1)} %bitcast.11.refs_2_.refs_0_), channel_id=1, source_target_pairs={{0,1},{1,0},{2,3},{3,2},{4,5},{5,4},{6,7},{7,6},{8,9},{9,8},{10,11... | collective-permute-start | bytes 7077896 | tf_op jit(solution)/shard_map/ppermute | solution.py:411
  75.4 29.2 %collective-permute-start.4 = (bf16[1536,768]{1,0:T(8,128)(2,1)}, bf16[1536,768]{1,0:T(8,128)(2,1)}, u32[]{:S(2)}, u32[]{:S(2)}) collective-permute-start(bf16[1536,768]{1,0:T(8,128)(2,1)} %bitcast.11.refs_2_.refs_0_), channel_id=1, source_target_pairs={{0,6},{2,0},{4,2},{6,4},{1,3},{3,5},{5,7},{7,1},{8,14},{10,8},{12,... | collective-permute-start | bytes 7077896 | tf_op jit(solution)/shard_map/ppermute | solution.py:408
  76.2 25.2 %all-to-all-start.2 = ((bf16[16,96,512]{2,1,0:T(8,128)(2,1)}), bf16[16,96,512]{2,1,0:T(8,128)(2,1)}, u32[]{:S(2)}, u32[]{:S(2)}) async-start(bf16[16,96,512]{2,1,0:T(8,128)(2,1)} %bitcast.35), calls=%async_computation.2 | async-start | bytes 3145728 | tf_op jit(solution)/shard_map/all_to_all | solution.py:404
  80.6 13.8 %copy-start.1 = (bf16[672,1536]{1,0:T(8,128)(2,1)S(1)}, bf16[672,1536]{1,0:T(8,128)(2,1)}, u32[]{:S(2)}) copy-start(bf16[672,1536]{1,0:T(8,128)(2,1)} %copy-done) | copy-start | bytes 6193156
  80.6 13.8 %copy-start.11 = (s32[3]{0:T(128)S(1)}, s32[3]{0:T(128)}, u32[]{:S(2)}) copy-start(s32[3]{0:T(128)} %copy-done.10) | copy-start | bytes 40
  104.6 24.7 %copy-start.12 = (s32[3]{0:T(128)S(1)}, s32[3]{0:T(128)}, u32[]{:S(2)}) copy-start(s32[3]{0:T(128)} %copy-done.10) | copy-start | bytes 40
  104.6 24.7 %collective-permute-start.6 = (bf16[1536,768]{1,0:T(8,128)(2,1)}, bf16[1536,768]{1,0:T(8,128)(2,1)}, u32[]{:S(2)}, u32[]{:S(2)}) collective-permute-start(bf16[1536,768]{1,0:T(8,128)(2,1)} %collective-permute-done.4.refs_0_), channel_id=1, source_target_pairs={{0,1},{1,0},{2,3},{3,2},{4,5},{5,4},{6,7},{7,6},{8,9},{9,8},{10,11... | collective-permute-start | bytes 7077896 | tf_op jit(solution)/shard_map/ppermute | solution.py:411
  105.4 23.9 %collective-permute-start.7 = (bf16[1536,512]{1,0:T(8,128)(2,1)}, bf16[1536,512]{1,0:T(8,128)(2,1)}, u32[]{:S(2)}, u32[]{:S(2)}) collective-permute-start(bf16[1536,512]{1,0:T(8,128)(2,1)} %bitcast.13.refs_2_), channel_id=1, source_target_pairs={{0,1},{1,0},{2,3},{3,2},{4,5},{5,4},{6,7},{7,6},{8,9},{9,8},{10,11... | collective-permute-start | bytes 4718600 | tf_op jit(solution)/shard_map/ppermute | solution.py:411
  121.9 19.1 %all-to-all-start.3 = ((f32[64,1,96]{2,1,0:T(1,128)}), f32[64,1,96]{2,1,0:T(1,128)S(1)}, u32[]{:S(2)}, u32[]{:S(2)}) async-start(f32[64,1,96]{2,1,0:T(1,128)} %bitcast.48), calls=%async_computation.3 | async-start | bytes 65536 | tf_op jit(solution)/shard_map/all_to_all | solution.py:438
  129.3 1.6 %copy-start.2 = (bf16[672,1536]{1,0:T(8,128)(2,1)S(1)}, bf16[672,1536]{1,0:T(8,128)(2,1)}, u32[]{:S(2)}) copy-start(bf16[672,1536]{1,0:T(8,128)(2,1)} %copy-done) | copy-start | bytes 6193156
  140.9 0.6 copy-start.17

commit v5 on v4

--- a/solution.py
+++ b/solution.py
@@ -14,6 +14,7 @@
 DIRECT = (1024, 512)
 TILE_FF = 336
 TILE_D = 256
+STEPS = 4
 SUB = 16
 COLS = 256
 VMEM_MB = {"dispatch": 16, "dispatch_more": 12, "activation": 16, "raw": 56, "finish": 56, "down": 20}
@@ -64,25 +65,33 @@
 
 
 def dispatch_kernel(experts, capacity, where_ref, route_ref, prob_ref, grad_ref,
-                    send_ref, slot_ref, pick_ref):
+                    send_ref, slot_ref, pick_ref, weight):
     top, tokens = route_ref.shape
-    expert = lax.broadcasted_iota(jnp.int32, (experts, tokens), 0)
-    chosen = jnp.zeros((experts, tokens), F32)
-    prob = jnp.zeros((experts, tokens), F32)
-    for k in range(top):
-        hit = route_ref[k : k + 1, :] == expert
-        chosen = jnp.where(hit, 1.0, chosen)
-        prob = jnp.where(hit, prob_ref[k : k + 1, :].astype(F32), prob)
-    row = lax.broadcasted_iota(jnp.int32, (tokens, tokens), 0)
-    col = lax.broadcasted_iota(jnp.int32, (tokens, tokens), 1)
-    earlier = (row < col).astype(BF16)
-    before = jnp.dot(chosen.astype(BF16), earlier, preferred_element_type=F32)
-    slot = jnp.where(chosen > 0.5, before, -1.0)
-    slot_ref[...] = slot
+    step = pl.program_id(0)
+    group = experts // pl.num_programs(0)
+
+    @pl.when(step == 0)
+    def _():
+        expert = lax.broadcasted_iota(jnp.int32, (experts, tokens), 0)
+        chosen = jnp.zeros((experts, tokens), F32)
+        prob = jnp.zeros((experts, tokens), F32)
+        for k in range(top):
+            hit = route_ref[k : k + 1, :] == expert
+            chosen = jnp.where(hit, 1.0, chosen)
+            prob = jnp.where(hit, prob_ref[k : k + 1, :].astype(F32), prob)
+        row = lax.broadcasted_iota(jnp.int32, (tokens, tokens), 0)
+        col = lax.broadcasted_iota(jnp.int32, (tokens, tokens), 1)
+        earlier = (row < col).astype(BF16)
+        before = jnp.dot(chosen.astype(BF16), earlier, preferred_element_type=F32)
+        slot = jnp.where(chosen > 0.5, before, -1.0)
+        slot_ref[...] = slot
+        weight[...] = prob
+
     place = lax.broadcasted_iota(jnp.int32, (capacity, tokens), 0).astype(F32)
-    for e in range(experts):
+    for e in range(group):
+        one = pl.ds(step * group + e, 1)
         pick_ref[pl.ds(e * capacity, capacity), :] = jnp.where(
-            slot[e : e + 1, :] == place, prob[e : e + 1, :], 0.0
+            slot_ref[one, :] == place, weight[one, :], 0.0
         ).astype(BF16)
     send_ref[...] = jnp.dot(
         pick_ref[...], grad_ref[...], preferred_element_type=F32
@@ -97,23 +106,23 @@
     return call(
         functools.partial(dispatch_kernel, experts, capacity),
         "dispatch",
-        (1,),
+        (STEPS,),
         [
             pl.BlockSpec(route.shape, fixed),
             pl.BlockSpec(prob.shape, fixed),
             pl.BlockSpec((tokens, part), lambda i, s: (0, at(s))),
         ],
         [
-            pl.BlockSpec((total, part), fixed),
+            pl.BlockSpec((total // STEPS, part), lambda i, s: (i, 0)),
             pl.BlockSpec((experts, tokens), fixed),
-            pl.BlockSpec((total, tokens), fixed),
+            pl.BlockSpec((total // STEPS, tokens), lambda i, s: (i, 0)),
         ],
         [
             jax.ShapeDtypeStruct((total, part), BF16),
             jax.ShapeDtypeStruct((experts, tokens), F32),
             jax.ShapeDtypeStruct((total, tokens), BF16),
         ],
-        [],
+        [pltpu.VMEM((experts, tokens), F32)],
         2 * total * tokens * part,
         2 * total * part,
     )(where, route, prob, grad)

time: 144 us -> 145 us (level)
  transfers between devices with their start and end apart: 12 -> 12, of which waited for: 4 -> 4; matrix products, arithmetic and copies ran while one was open for 0% -> 0% of each run, Pallas kernels for 44% -> 43%
where the time goes in v5:
time: 145 us; the launch traced here: 144 us
  Pallas kernels  65.6 us (45%)
  starting transfers between devices  43.4 us (30%)
  waiting for transfers between devices  19.8 us (14%)
  local copies, waits for them, and re-layouts  14.3 us (10%)
    pallas_call x4, Pallas kernels, down(): call(functools.partial(down_kernel, counts), 'down', (tiles,), in_specs,...  26.7 us
    all_to_all x3, starting transfers between devices, fetch(): x = lax.all_to_all(x, 'expert', split_axis=0, concat_axis=0, tiled=True)  18.5 us
    pallas_call x1, Pallas kernels, finish(): call(functools.partial(finish_kernel, len(pieces)), 'finish', (ff // TILE...  16.4 us
    ppermute x6, starting transfers between devices, swap_dp(): return lax.ppermute(x, 'dp', [(0, 1), (1, 0)])  15.4 us
    unnamed x36, local copies, waits for them, and re-layouts  14.3 us
    pallas_call x1, Pallas kernels, raw_part(): call(functools.partial(raw_kernel, len(pieces), more), 'raw', (ff // TILE...  13.8 us
    ppermute x2, waiting for transfers between devices, beside(): return lax.ppermute(x, ('etp', 'dp'), swap)  12.8 us
    all_to_all x1, starting transfers between devices, local(): lax.all_to_all(sums, ('etp', 'expert'), split_axis=0, concat_axis=0, tile...  7.49 us
  transfers between devices with their start and end apart: 12, of which 4 were waited for; matrix products, arithmetic and copies ran while one was open for 0% of the time, Pallas kernels for 43%

profile of v5, /device:TPU:1, one launch (start us, length us, event | category | flops | bytes accessed | tf_op | source)
XLA Modules:
  0.0 144.1 jit_solution(7920027046646909645)
XLA Ops:
  0.6 1.4 copy-done.5
  3.4 1.3 dispatch.1
  4.7 1.1 copy-done.9
  5.9 8.6 %all-to-all-start = ((bf16[16,96,512]{2,1,0:T(8,128)(2,1)}), bf16[16,96,512]{2,1,0:T(8,128)(2,1)}, u32[]{:S(2)}, u32[]{:S(2)}) async-start(bf16[16,96,512]{2,1,0:T(8,128)(2,1)} %bitcast.36), calls=%async_computation | async-start | bytes 3145728 | tf_op jit(solution)/shard_map/all_to_all | solution.py:413
  14.5 1.0 dispatch_more.2
  15.6 1.4 copy-done.7
  17.0 0.8 dispatch_more.3
  17.8 1.2 copy-done.8
  19.0 2.2 %copy-done.3 = bf16[1,1536,1344]{1,2,0:T(8,128)(2,1)S(1)} copy-done((bf16[1,1536,1344]{1,2,0:T(8,128)(2,1)S(1)}, bf16[1,1536,1344]{1,2,0:T(8,128)(2,1)}, u32[]{:S(2)}) %copy-start.3) | copy-done | bytes 4128792
  21.2 2.2 %copy-done.4 = bf16[1,1536,1344]{1,2,0:T(8,128)(2,1)S(1)} copy-done((bf16[1,1536,1344]{1,2,0:T(8,128)(2,1)S(1)}, bf16[1,1536,1344]{1,2,0:T(8,128)(2,1)}, u32[]{:S(2)}) %copy-start.4) | copy-done | bytes 4128792
  23.3 3.8 %activation.1 = (bf16[672,1536]{1,0:T(8,128)(2,1)S(1)}, bf16[672,1536]{1,0:T(8,128)(2,1)S(1)}) custom-call(s32[3]{0:T(128)S(1)} %pad_add_fusion.where_ref, bf16[1344,1536]{1,0:T(8,128)(2,1)S(1)} %bitcast.31, bf16[1344,1536]{1,0:T(8,128)(2,1)S(1)} %bitcast.33), custom_call_target="tpu_custom_call" | custom-call | flops 1 | bytes 1 | tf_op jit(solution)/shard_map/activation/pallas_call | solution.py:191
  27.2 1.3 copy-done.16
  28.4 6.7 %all-to-all-done = bf16[16,96,512]{2,1,0:T(8,128)(2,1)} async-done(((bf16[16,96,512]{2,1,0:T(8,128)(2,1)}), bf16[16,96,512]{2,1,0:T(8,128)(2,1)}, u32[]{:S(2)}, u32[]{:S(2)}) %all-to-all-start) | async-done | bytes 1572896 | tf_op jit(solution)/shard_map/all_to_all | solution.py:413
  35.2 1.2 collective-permute-start.1
  36.4 5.4 %all-to-all-start.1 = ((bf16[16,96,768]{2,1,0:T(8,128)(2,1)}), bf16[16,96,768]{2,1,0:T(8,128)(2,1)}, u32[]{:S(2)}, u32[]{:S(2)}) async-start(bf16[16,96,768]{2,1,0:T(8,128)(2,1)} %bitcast.34), calls=%async_computation.1 | async-start | bytes 4718592 | tf_op jit(solution)/shard_map/all_to_all | solution.py:413
  41.8 4.8 %collective-permute-start = (bf16[672,1536]{1,0:T(8,128)(2,1)}, bf16[672,1536]{1,0:T(8,128)(2,1)S(1)}, u32[]{:S(2)}, u32[]{:S(2)}) collective-permute-start(bf16[672,1536]{1,0:T(8,128)(2,1)} %copy-done.16), channel_id=1, source_target_pairs={{0,1},{1,0},{2,3},{3,2},{4,5},{5,4},{6,7},{7,6},{8,9},{9,8},{10,11... | collective-permute-start | bytes 6193160 | tf_op jit(solution)/shard_map/ppermute | solution.py:420
  46.7 9.6 %collective-permute-done.1.refs_0_.refs_4_ = bf16[1536,512]{1,0:T(8,128)(2,1)} collective-permute-done((bf16[1536,512]{1,0:T(8,128)(2,1)}, bf16[1536,512]{1,0:T(8,128)(2,1)}, u32[]{:S(2)}, u32[]{:S(2)}) %collective-permute-start.1) | collective-permute-done | bytes 1572896 | tf_op jit(solution)/shard_map/ppermute | solution.py:417
  56.3 4.0 %collective-permute-start.2 = (bf16[1536,512]{1,0:T(8,128)(2,1)}, bf16[1536,512]{1,0:T(8,128)(2,1)S(1)}, u32[]{:S(2)}, u32[]{:S(2)}) collective-permute-start(bf16[1536,512]{1,0:T(8,128)(2,1)} %collective-permute-done.1.refs_0_.refs_4_), channel_id=1, source_target_pairs={{0,1},{1,0},{2,3},{3,2},{4,5},{5,4},{6,7},{7,6},{8,9},{9,8},{10,11... | collective-permute-start | bytes 4718600 | tf_op jit(solution)/shard_map/ppermute | solution.py:420
  60.3 5.1 %down.4.refs_2_ = bf16[672,3072]{1,0:T(8,128)(2,1)} custom-call(s32[3]{0:T(128)S(1)} %pad_add_fusion.where_ref, bf16[672,1536]{1,0:T(8,128)(2,1)S(1)} %get-tuple-element.38.here_ref, bf16[672,1536]{1,0:T(8,128)(2,1)S(1)} %collective-permute-done.there_ref, bf16[1536,512]{1,0:T(8,128)(2,1)} %bitcast.9.refs_0_, ...), custom_call_target="tpu_custom_call" | custom-call | flops 528482304 | bytes 1990656 | tf_op jit(solution)/shard_map/down/pallas_call | solution.py:357
  65.4 4.9 %down.5.refs_2_ = bf16[672,3072]{1,0:T(8,128)(2,1)} custom-call(s32[3]{0:T(128)S(1)} %pad_add_fusion.where_ref, bf16[672,1536]{1,0:T(8,128)(2,1)S(1)} %get-tuple-element.38.here_ref, bf16[672,1536]{1,0:T(8,128)(2,1)S(1)} %collective-permute-done.there_ref, bf16[1536,512]{1,0:T(8,128)(2,1)} %collective-permute-done.1.refs_0_.refs_4_, ...), custom_call_target="tpu_custom_call", output_to_operand_aliasing={{}: (5, {})} | custom-call | flops 528482304 | bytes 1990656 | tf_op jit(solution)/shard_map/down/pallas_call | solution.py:357
  70.3 5.5 %collective-permute-start.5 = (bf16[1536,768]{1,0:T(8,128)(2,1)}, bf16[1536,768]{1,0:T(8,128)(2,1)}, u32[]{:S(2)}, u32[]{:S(2)}) collective-permute-start(bf16[1536,768]{1,0:T(8,128)(2,1)} %bitcast.11.refs_2_.refs_0_), channel_id=1, source_target_pairs={{0,1},{1,0},{2,3},{3,2},{4,5},{5,4},{6,7},{7,6},{8,9},{9,8},{10,11... | collective-permute-start | bytes 7077896 | tf_op jit(solution)/shard_map/ppermute | solution.py:420
  75.9 0.9 collective-permute-start.4
  76.8 4.4 %all-to-all-start.2 = ((bf16[16,96,512]{2,1,0:T(8,128)(2,1)}), bf16[16,96,512]{2,1,0:T(8,128)(2,1)}, u32[]{:S(2)}, u32[]{:S(2)}) async-start(bf16[16,96,512]{2,1,0:T(8,128)(2,1)} %bitcast.35), calls=%async_computation.2 | async-start | bytes 3145728 | tf_op jit(solution)/shard_map/all_to_all | solution.py:413
  81.2 13.8 %raw.1.before_ref = f32[1344,1536]{1,0:T(8,128)} custom-call(s32[3]{0:T(128)} %copy-done.10, bf16[1536,512]{1,0:T(8,128)(2,1)} %bitcast.9.refs_0_, bf16[1344,3072]{1,0:T(8,128)(2,1)} %bitcast.41, bf16[1536,768]{1,0:T(8,128)(2,1)} %bitcast.11.refs_2_.refs_0_, bf16[1344,3072]{1,0:T(8,128)(2,1)} %bitcast.42, ...), custom_call_target="tpu_custom_call" | custom-call | flops 1849688064 | bytes 6709248 | tf_op jit(solution)/shard_map/raw/pallas_call | solution.py:244
  95.0 6.7 %down.6.refs_4_ = bf16[672,3072]{1,0:T(8,128)(2,1)} custom-call(s32[3]{0:T(128)S(1)} %copy-done.11, bf16[672,1536]{1,0:T(8,128)(2,1)S(1)} %get-tuple-element.38.here_ref, bf16[672,1536]{1,0:T(8,128)(2,1)S(1)} %copy-done.1, bf16[1536,768]{1,0:T(8,128)(2,1)} %bitcast.11.refs_2_.refs_0_, ...), custom_call_target="tpu_custom_call", output_to_operand_aliasing={{}: (5, {})} | custom-call | flops 792723456 | bytes 2469888 | tf_op jit(solution)/shard_map/down/pallas_call | solution.py:357
  101.9 3.2 %collective-permute-done.4.refs_0_ = bf16[1536,768]{1,0:T(8,128)(2,1)} collective-permute-done((bf16[1536,768]{1,0:T(8,128)(2,1)}, bf16[1536,768]{1,0:T(8,128)(2,1)}, u32[]{:S(2)}, u32[]{:S(2)}) %collective-permute-start.4) | collective-permute-done | bytes 2359328 | tf_op jit(solution)/shard_map/ppermute | solution.py:417
  105.1 0.8 collective-permute-start.6
  106.0 16.4 %finish.1 = (bf16[1344,1536]{1,0:T(8,128)(2,1)}, bf16[1344,1536]{1,0:T(8,128)(2,1)}, f32[4,16,96]{2,1,0:T(8,128)}) custom-call(s32[3]{0:T(128)} %copy-done.10, bf16[1344,1536]{1,0:T(8,128)(2,1)} %bitcast.30, bf16[1344,1536]{1,0:T(8,128)(2,1)} %bitcast.32, f32[1344,1536]{1,0:T(8,128)} %raw.1.before_ref, bf16[1536,768]{1,0:T(8,128)(2,1)} %collective-permute-done.4.refs_0_, ...), custom_call_target="tpu_custom_call" | custom-call | flops 1321205760 | bytes 8036352 | tf_op jit(solution)/shard_map/finish/pallas_call | solution.py:301
  122.5 7.5 %all-to-all-start.3 = ((f32[64,1,96]{2,1,0:T(1,128)}), f32[64,1,96]{2,1,0:T(1,128)S(1)}, u32[]{:S(2)}, u32[]{:S(2)}) async-start(f32[64,1,96]{2,1,0:T(1,128)} %bitcast.48), calls=%async_computation.3 | async-start | bytes 65536 | tf_op jit(solution)/shard_map/all_to_all | solution.py:447
  130.0 1.6 %copy-done.2 = bf16[672,1536]{1,0:T(8,128)(2,1)S(1)} copy-done((bf16[672,1536]{1,0:T(8,128)(2,1)S(1)}, bf16[672,1536]{1,0:T(8,128)(2,1)}, u32[]{:S(2)}) %copy-start.2) | copy-done | bytes 2064408
  131.6 10.0 %down.7 = bf16[672,3072]{1,0:T(8,128)(2,1)} custom-call(s32[3]{0:T(128)S(1)} %copy-done.12, bf16[672,1536]{1,0:T(8,128)(2,1)S(1)} %get-tuple-element.38.here_ref, bf16[672,1536]{1,0:T(8,128)(2,1)S(1)} %copy-done.2, bf16[1536,768]{1,0:T(8,128)(2,1)} %collective-permute-done.4.refs_0_, ...), custom_call_target="tpu_custom_call", output_to_operand_aliasing={{}: (7, {})} | custom-call | flops 1321205760 | bytes 3428352 | tf_op jit(solution)/shard_map/down/pallas_call | solution.py:357
  142.2 1.8 %combine.1 = f32[4,256]{1,0:T(4,128)} custom-call(s32[4,256]{1,0:T(4,128)} %bitcast.37, bf16[4,256]{1,0:T(4,128)(2,1)} %bitcast.39, f32[16,256]{1,0:T(8,128)} %copy-done.14, f32[4,16,96]{2,1,0:T(8,128)} %bitcast.47), custom_call_target="tpu_custom_call" | custom-call | tf_op jit(solution)/shard_map/combine/pallas_call | solution.py:390
  (40 shorter events, 2.6 us)
Async XLA Ops:
  0.6 1.4 copy-start.5
  2.0 0.7 copy-start.13
  2.7 0.7 copy-start.15
  3.4 11.1 %copy-start.6 = (bf16[256,3072]{1,0:T(8,128)(2,1)S(1)}, bf16[256,3072]{1,0:T(8,128)(2,1)}, u32[]{:S(2)}) copy-start(bf16[256,3072]{1,0:T(8,128)(2,1)} %grad_ref.5) | copy-start | bytes 4718596
  4.7 1.1 copy-start.9
  5.9 8.7 %copy-start.14 = (f32[16,256]{1,0:T(8,128)}, f32[16,256]{1,0:T(8,128)S(1)}, u32[]{:S(2)}) copy-start(f32[16,256]{1,0:T(8,128)S(1)} %get-tuple-element.52.slot_ref) | copy-start | bytes 49156
  5.9 29.3 %all-to-all-start = ((bf16[16,96,512]{2,1,0:T(8,128)(2,1)}), bf16[16,96,512]{2,1,0:T(8,128)(2,1)}, u32[]{:S(2)}, u32[]{:S(2)}) async-start(bf16[16,96,512]{2,1,0:T(8,128)(2,1)} %bitcast.36), calls=%async_computation | async-start | bytes 3145728 | tf_op jit(solution)/shard_map/all_to_all | solution.py:413
  15.6 1.4 copy-start.7
  17.7 1.2 copy-start.8
  19.0 2.2 %copy-start.3 = (bf16[1,1536,1344]{1,2,0:T(8,128)(2,1)S(1)}, bf16[1,1536,1344]{1,2,0:T(8,128)(2,1)}, u32[]{:S(2)}) copy-start(bf16[1,1536,1344]{1,2,0:T(8,128)(2,1)} %param.10) | copy-start | bytes 12386308
  21.2 2.2 %copy-start.4 = (bf16[1,1536,1344]{1,2,0:T(8,128)(2,1)S(1)}, bf16[1,1536,1344]{1,2,0:T(8,128)(2,1)}, u32[]{:S(2)}) copy-start(bf16[1,1536,1344]{1,2,0:T(8,128)(2,1)} %param.11) | copy-start | bytes 12386308
  23.3 42.1 %copy-start.10 = (s32[3]{0:T(128)}, s32[3]{0:T(128)S(1)}, u32[]{:S(2)}) copy-start(s32[3]{0:T(128)S(1)} %pad_add_fusion.where_ref) | copy-start | bytes 40
  27.1 1.3 copy-start.16
  35.2 21.1 %collective-permute-start.1 = (bf16[1536,512]{1,0:T(8,128)(2,1)}, bf16[1536,512]{1,0:T(8,128)(2,1)}, u32[]{:S(2)}, u32[]{:S(2)}) collective-permute-start(bf16[1536,512]{1,0:T(8,128)(2,1)} %bitcast.9.refs_0_), channel_id=1, source_target_pairs={{0,6},{2,0},{4,2},{6,4},{1,3},{3,5},{5,7},{7,1},{8,14},{10,8},{12,... | collective-permute-start | bytes 4718600 | tf_op jit(solution)/shard_map/ppermute | solution.py:417
  36.4 34.0 %all-to-all-start.1 = ((bf16[16,96,768]{2,1,0:T(8,128)(2,1)}), bf16[16,96,768]{2,1,0:T(8,128)(2,1)}, u32[]{:S(2)}, u32[]{:S(2)}) async-start(bf16[16,96,768]{2,1,0:T(8,128)(2,1)} %bitcast.34), calls=%async_computation.1 | async-start | bytes 4718592 | tf_op jit(solution)/shard_map/all_to_all | solution.py:413
  41.8 18.5 %collective-permute-start = (bf16[672,1536]{1,0:T(8,128)(2,1)}, bf16[672,1536]{1,0:T(8,128)(2,1)S(1)}, u32[]{:S(2)}, u32[]{:S(2)}) collective-permute-start(bf16[672,1536]{1,0:T(8,128)(2,1)} %copy-done.16), channel_id=1, source_target_pairs={{0,1},{1,0},{2,3},{3,2},{4,5},{5,4},{6,7},{7,6},{8,9},{9,8},{10,11... | collective-permute-start | bytes 6193160 | tf_op jit(solution)/shard_map/ppermute | solution.py:420
  46.6 13.7 %collective-permute-start.3 = (bf16[1536,512]{1,0:T(8,128)(2,1)}, bf16[1536,512]{1,0:T(8,128)(2,1)S(1)}, u32[]{:S(2)}, u32[]{:S(2)}) collective-permute-start(bf16[1536,512]{1,0:T(8,128)(2,1)} %bitcast.9.refs_0_), channel_id=1, source_target_pairs={{0,1},{1,0},{2,3},{3,2},{4,5},{5,4},{6,7},{7,6},{8,9},{9,8},{10,11... | collective-permute-start | bytes 4718600 | tf_op jit(solution)/shard_map/ppermute | solution.py:420
  56.3 9.1 %collective-permute-start.2 = (bf16[1536,512]{1,0:T(8,128)(2,1)}, bf16[1536,512]{1,0:T(8,128)(2,1)S(1)}, u32[]{:S(2)}, u32[]{:S(2)}) collective-permute-start(bf16[1536,512]{1,0:T(8,128)(2,1)} %collective-permute-done.1.refs_0_.refs_4_), channel_id=1, source_target_pairs={{0,1},{1,0},{2,3},{3,2},{4,5},{5,4},{6,7},{7,6},{8,9},{9,8},{10,11... | collective-permute-start | bytes 4718600 | tf_op jit(solution)/shard_map/ppermute | solution.py:420
  60.3 5.1 %copy-start = (bf16[672,1536]{1,0:T(8,128)(2,1)}, bf16[672,1536]{1,0:T(8,128)(2,1)S(1)}, u32[]{:S(2)}) copy-start(bf16[672,1536]{1,0:T(8,128)(2,1)S(1)} %collective-permute-done.there_ref) | copy-start | bytes 6193156
  70.3 24.6 %collective-permute-start.5 = (bf16[1536,768]{1,0:T(8,128)(2,1)}, bf16[1536,768]{1,0:T(8,128)(2,1)}, u32[]{:S(2)}, u32[]{:S(2)}) collective-permute-start(bf16[1536,768]{1,0:T(8,128)(2,1)} %bitcast.11.refs_2_.refs_0_), channel_id=1, source_target_pairs={{0,1},{1,0},{2,3},{3,2},{4,5},{5,4},{6,7},{7,6},{8,9},{9,8},{10,11... | collective-permute-start | bytes 7077896 | tf_op jit(solution)/shard_map/ppermute | solution.py:420
  75.9 29.2 %collective-permute-start.4 = (bf16[1536,768]{1,0:T(8,128)(2,1)}, bf16[1536,768]{1,0:T(8,128)(2,1)}, u32[]{:S(2)}, u32[]{:S(2)}) collective-permute-start(bf16[1536,768]{1,0:T(8,128)(2,1)} %bitcast.11.refs_2_.refs_0_), channel_id=1, source_target_pairs={{0,6},{2,0},{4,2},{6,4},{1,3},{3,5},{5,7},{7,1},{8,14},{10,8},{12,... | collective-permute-start | bytes 7077896 | tf_op jit(solution)/shard_map/ppermute | solution.py:417
  76.8 25.2 %all-to-all-start.2 = ((bf16[16,96,512]{2,1,0:T(8,128)(2,1)}), bf16[16,96,512]{2,1,0:T(8,128)(2,1)}, u32[]{:S(2)}, u32[]{:S(2)}) async-start(bf16[16,96,512]{2,1,0:T(8,128)(2,1)} %bitcast.35), calls=%async_computation.2 | async-start | bytes 3145728 | tf_op jit(solution)/shard_map/all_to_all | solution.py:413
  81.2 13.8 %copy-start.1 = (bf16[672,1536]{1,0:T(8,128)(2,1)S(1)}, bf16[672,1536]{1,0:T(8,128)(2,1)}, u32[]{:S(2)}) copy-start(bf16[672,1536]{1,0:T(8,128)(2,1)} %copy-done) | copy-start | bytes 6193156
  81.2 13.8 %copy-start.11 = (s32[3]{0:T(128)S(1)}, s32[3]{0:T(128)}, u32[]{:S(2)}) copy-start(s32[3]{0:T(128)} %copy-done.10) | copy-start | bytes 40
  105.1 24.9 %copy-start.12 = (s32[3]{0:T(128)S(1)}, s32[3]{0:T(128)}, u32[]{:S(2)}) copy-start(s32[3]{0:T(128)} %copy-done.10) | copy-start | bytes 40
  105.1 24.9 %collective-permute-start.6 = (bf16[1536,768]{1,0:T(8,128)(2,1)}, bf16[1536,768]{1,0:T(8,128)(2,1)}, u32[]{:S(2)}, u32[]{:S(2)}) collective-permute-start(bf16[1536,768]{1,0:T(8,128)(2,1)} %collective-permute-done.4.refs_0_), channel_id=1, source_target_pairs={{0,1},{1,0},{2,3},{3,2},{4,5},{5,4},{6,7},{7,6},{8,9},{9,8},{10,11... | collective-permute-start | bytes 7077896 | tf_op jit(solution)/shard_map/ppermute | solution.py:420
  105.9 24.0 %collective-permute-start.7 = (bf16[1536,512]{1,0:T(8,128)(2,1)}, bf16[1536,512]{1,0:T(8,128)(2,1)}, u32[]{:S(2)}, u32[]{:S(2)}) collective-permute-start(bf16[1536,512]{1,0:T(8,128)(2,1)} %bitcast.13.refs_2_), channel_id=1, source_target_pairs={{0,1},{1,0},{2,3},{3,2},{4,5},{5,4},{6,7},{7,6},{8,9},{9,8},{10,11... | collective-permute-start | bytes 4718600 | tf_op jit(solution)/shard_map/ppermute | solution.py:420
  122.5 19.2 %all-to-all-start.3 = ((f32[64,1,96]{2,1,0:T(1,128)}), f32[64,1,96]{2,1,0:T(1,128)S(1)}, u32[]{:S(2)}, u32[]{:S(2)}) async-start(f32[64,1,96]{2,1,0:T(1,128)} %bitcast.48), calls=%async_computation.3 | async-start | bytes 65536 | tf_op jit(solution)/shard_map/all_to_all | solution.py:447
  130.0 1.6 %copy-start.2 = (bf16[672,1536]{1,0:T(8,128)(2,1)S(1)}, bf16[672,1536]{1,0:T(8,128)(2,1)}, u32[]{:S(2)}) copy-start(bf16[672,1536]{1,0:T(8,128)(2,1)} %copy-done) | copy-start | bytes 6193156
  141.6 0.6 copy-start.17
